TPU v7x, 32 devices: a whole 2x2x4 slice. The times are simulated.
32 devices in a mesh: dp: 16 (over z, y, x), blk: 2 (over core).
Axes of the slice: x: 2, y: 2, z: 4, core: 2. Of those that a mesh axis runs over, the one named last changes fastest.
Arguments:
- token_ids: int32 [32, 1024], P('dp', 'blk'), may hold values from 0 to 31999
- seq_lengths: int32 [32], P('dp'), may hold values from 32 to 1024, as said below
- diffusion_time: int32 [32], P('dp'), may hold values from 1 to 300
- embed_table: bfloat16 [32000, 256], replicated, may hold values from -6 to 6
- w_embed: bfloat16 [256, 1024], replicated, may hold values from -0.375 to 0.375
- w_time: bfloat16 [256, 4096], replicated, may hold values from -0.1875 to 0.1875
- gain_attn: float32 [1024], replicated, may hold values from 0.1 to 1.9
- bias_attn: float32 [1024], replicated, may hold values from -3 to 3
- gain_mlp: float32 [1024], replicated, may hold values from 0.1 to 1.9
- bias_mlp: float32 [1024], replicated, may hold values from -3 to 3
- w_qkv: bfloat16 [1024, 3072], replicated, may hold values from -0.1875 to 0.1875
- w_out: bfloat16 [1024, 1024], replicated, may hold values from -0.75 to 0.75
- w_up: bfloat16 [1024, 4096], replicated, may hold values from -0.1875 to 0.1875
- w_down: bfloat16 [4096, 1024], replicated, may hold values from -0.09375 to 0.09375
- cotangent: bfloat16 [32, 1024, 1024], P('dp', 'blk'), may hold values from -6 to 6
Outputs:
- layer_out: bfloat16 [32, 1024, 1024], P('dp', 'blk')
- grad_input: bfloat16 [32, 1024, 1024], P('dp', 'blk')
- grad_table: float32 [32000, 256], P(('dp', 'blk'))
- grad_w_embed: float32 [256, 1024], P(None, ('dp', 'blk'))
- grad_w_time: float32 [256, 4096], P(None, ('dp', 'blk'))
- grad_gain_attn: float32 [1024], P(('dp', 'blk'))
- grad_bias_attn: float32 [1024], P(('dp', 'blk'))
- grad_gain_mlp: float32 [1024], P(('dp', 'blk'))
- grad_bias_mlp: float32 [1024], P(('dp', 'blk'))
- grad_w_qkv: float32 [1024, 3072], P(None, ('dp', 'blk'))
- grad_w_out: float32 [1024, 1024], P(None, ('dp', 'blk'))
- grad_w_up: float32 [1024, 4096], P(None, ('dp', 'blk'))
- grad_w_down: float32 [4096, 1024], P(None, ('dp', 'blk'))
Inputs may be any that keep to these rules, and one draw needn't show every extreme that they name: `seq_lengths`: of the 2 sequences of one index of dp, one has exactly 1024 real tokens; positions at or past a sequence's length are padding.
All inputs are finite; a program needn't handle non-finite values.
Results may differ from a plain program's by a relative error of at most 0.02.
Values may be sent and summed in bfloat16 or wider, within the bound.
No kernel may reach another device: no remote copies, remote signals or barrier semaphores. Data moves between devices by JAX's collectives and lax.ppermute only.
A program may use at most 384 MiB of HBM per device.

v0:
```python
import math

import jax
import jax.numpy as jnp
from jax import lax
from jax.sharding import PartitionSpec as P

D = 1024
HEADS = 16
HEAD_DIM = 64
EMB = 256
VOCAB = 32000
TIME_WIDTH = 256


NEG_FILL = -1000000000.0


def from_behind(value, axis, steps):
    count = lax.axis_size(axis)
    pairs = [(source, (source + steps) % count) for source in range(count)]
    return lax.ppermute(value, axis, pairs)


def time_features(diffusion_time, feature_width):
    half_width = feature_width // 2
    frequency = jnp.exp(-math.log(1000.0) * jnp.arange(half_width, dtype=jnp.float32) / half_width)
    angles = diffusion_time.astype(jnp.float32)[:, None] * frequency[None, :]
    return jnp.concatenate([jnp.sin(angles), jnp.cos(angles)], axis=1)


def modulated_norm(features, gain_vec, bias_vec, scale_rows, shift_rows):
    center = features - jnp.mean(features, axis=-1, keepdims=True)
    spread = jnp.mean(center * center, axis=-1, keepdims=True)
    return center * lax.rsqrt(spread + 1e-05) * (gain_vec + scale_rows[:, None, :]) + (
        bias_vec + shift_rows[:, None, :]
    )


def normalize_rows(row_values):
    return row_values * lax.rsqrt(jnp.mean(row_values * row_values, axis=-1, keepdims=True) + 1e-06)


def project(left_side, right_side):
    return lax.dot_general(
        left_side,
        right_side,
        (((left_side.ndim - 1,), (0,)), ((), ())),
        preferred_element_type=jnp.float32,
    )


def project_back(left_side, right_side):
    return lax.dot_general(
        left_side,
        right_side,
        (((left_side.ndim - 1,), (1,)), ((), ())),
        preferred_element_type=jnp.float32,
    )


def outer_sum(left_side, right_side):
    return lax.dot_general(
        left_side, right_side, (((0, 1), (0, 1)), ((), ())), preferred_element_type=jnp.float32
    )


def scatter_rows(running_total, offsets, grad_values):
    row_span = running_total.shape[0]
    inside = (offsets >= 0) & (offsets < row_span)
    return running_total.at[jnp.where(inside, offsets, row_span)].add(grad_values, mode="drop")


def group_columns(matrix, group_count):
    if matrix.ndim == 1:
        return matrix.reshape(1, group_count, matrix.shape[0] // group_count)
    return matrix.reshape(matrix.shape[0], group_count, matrix.shape[1] // group_count)


def shards(
    token_ids,
    seq_lengths,
    diffusion_time,
    embed_table,
    w_embed,
    w_time,
    gain_attn,
    bias_attn,
    gain_mlp,
    bias_mlp,
    w_qkv,
    w_out,
    w_up,
    w_down,
    cotangent,
):
    seq_count, pos_count = token_ids.shape
    scale_factor = HEAD_DIM ** (-0.5)
    cycle_size = lax.axis_size("blk")
    cycle_index = lax.axis_index("blk")
    positions = cycle_index * pos_count + jnp.arange(pos_count, dtype=jnp.int32)
    valid_rows = (positions[None, :] < seq_lengths[:, None]).astype(jnp.float32)[:, :, None]
    emb_rows = embed_table[token_ids].astype(jnp.float32)
    normed, norm_pull = jax.vjp(normalize_rows, emb_rows)
    normed_low = normed.astype(jnp.bfloat16)
    inputs = project(normed_low, w_embed)
    time_low = time_features(diffusion_time, TIME_WIDTH).astype(jnp.bfloat16)
    modulation = jnp.dot(time_low, w_time, preferred_element_type=jnp.float32)
    scale_attn, shift_attn, scale_mlp, shift_mlp = jnp.split(modulation, 4, axis=1)
    normed_attn, attn_pull = jax.vjp(
        modulated_norm, inputs, gain_attn, bias_attn, scale_attn, shift_attn
    )
    attn_low = normed_attn.astype(jnp.bfloat16)
    qkv_low = project(attn_low, w_qkv).astype(jnp.bfloat16)
    queries = qkv_low[:, :, :D].reshape(seq_count, pos_count, HEADS, HEAD_DIM)
    kv_local = qkv_low[:, :, D:]

    def masked_scores(key_heads, key_start):
        key_count = key_heads.shape[1]
        key_pos = key_start + jnp.arange(key_count, dtype=jnp.int32)
        key_keep = (key_pos[None, :] < seq_lengths[:, None])[:, None, None, :]
        scores = (
            jnp.einsum("sqhd,skhd->shqk", queries, key_heads, preferred_element_type=jnp.float32)
            * scale_factor
        )
        return jnp.where(key_keep, scores, NEG_FILL)

    key_piece = lax.all_gather(kv_local, "blk", axis=1, tiled=True)
    run_max = jnp.full((seq_count, HEADS, pos_count), -1e30, jnp.float32)
    key_count = key_piece.shape[1]
    key_heads = key_piece[:, :, :D].reshape(seq_count, key_count, HEADS, HEAD_DIM)
    value_heads = key_piece[:, :, D:].reshape(seq_count, key_count, HEADS, HEAD_DIM)
    scores = masked_scores(key_heads, jnp.int32(0))
    new_max = jnp.maximum(run_max, jnp.max(scores, axis=-1))
    softmax_weights = jnp.exp(scores - new_max[..., None])
    run_sum = jnp.sum(softmax_weights, axis=-1)
    contrib = jnp.einsum(
        "shqk,skhd->sqhd",
        softmax_weights.astype(jnp.bfloat16),
        value_heads,
        preferred_element_type=jnp.float32,
    )
    run_acc = contrib
    run_max, run_sum, run_acc = (new_max, run_sum, run_acc)
    log_total = run_max + jnp.log(run_sum)
    attended = run_acc / jnp.transpose(run_sum, (0, 2, 1))[..., None]
    attended_low = attended.reshape(seq_count, pos_count, D).astype(jnp.bfloat16)
    residual = inputs + project(attended_low, w_out)
    normed_mlp, mlp_pull = jax.vjp(
        modulated_norm, residual, gain_mlp, bias_mlp, scale_mlp, shift_mlp
    )
    mlp_low = normed_mlp.astype(jnp.bfloat16)
    pre_act = project(mlp_low, w_up)
    activated, gelu_pull = jax.vjp(jax.nn.gelu, pre_act)
    hidden_low = activated.astype(jnp.bfloat16)
    final_sum = (residual + project(hidden_low, w_down)) * valid_rows
    layer_out = final_sum.astype(jnp.bfloat16)
    grad_final = cotangent.astype(jnp.float32) * valid_rows
    final_low = grad_final.astype(jnp.bfloat16)
    grad_w_down = outer_sum(hidden_low, final_low)
    (grad_pre,) = gelu_pull(project_back(final_low, w_down))
    pre_low = grad_pre.astype(jnp.bfloat16)
    grad_w_up = outer_sum(mlp_low, pre_low)
    grad_res_norm, grad_gain_mlp, grad_bias_mlp, grad_scale_mlp, grad_shift_mlp = mlp_pull(
        project_back(pre_low, w_up)
    )
    residual_grad = grad_final + grad_res_norm
    residual_low = residual_grad.astype(jnp.bfloat16)
    grad_w_out = outer_sum(attended_low, residual_low)
    grad_att = (
        project_back(residual_low, w_out)
        .astype(jnp.bfloat16)
        .reshape(seq_count, pos_count, HEADS, HEAD_DIM)
    )
    row_delta = jnp.transpose(jnp.sum(grad_att * attended, axis=-1), (0, 2, 1))

    def key_block(kv_block, owner_index):
        key_heads = kv_block[:, :, :D].reshape(seq_count, pos_count, HEADS, HEAD_DIM)
        value_heads = kv_block[:, :, D:].reshape(seq_count, pos_count, HEADS, HEAD_DIM)
        scores = masked_scores(key_heads, owner_index * pos_count)
        softmax_weights = jnp.exp(scores - log_total[..., None])
        grad_weights = jnp.einsum(
            "sqhd,skhd->shqk", grad_att, value_heads, preferred_element_type=jnp.float32
        )
        grad_scores = (
            softmax_weights * (grad_weights - row_delta[..., None]) * scale_factor
        ).astype(jnp.bfloat16)
        grad_queries = jnp.einsum(
            "shqk,skhd->sqhd", grad_scores, key_heads, preferred_element_type=jnp.float32
        )
        grad_keys = jnp.einsum(
            "shqk,sqhd->skhd", grad_scores, queries, preferred_element_type=jnp.float32
        )
        grad_values = jnp.einsum(
            "shqk,sqhd->skhd",
            softmax_weights.astype(jnp.bfloat16),
            grad_att,
            preferred_element_type=jnp.float32,
        )
        joined = jnp.concatenate(
            [
                grad_keys.reshape(seq_count, pos_count, D),
                grad_values.reshape(seq_count, pos_count, D),
            ],
            axis=-1,
        )
        return (grad_queries, joined)

    def pass_back(grad_values):
        return from_behind(grad_values.astype(jnp.bfloat16), "blk", 1).astype(grad_values.dtype)

    zero_kv = jnp.zeros((seq_count, pos_count, 2 * D), jnp.float32)
    zero_query = jnp.zeros((seq_count, pos_count, HEADS, HEAD_DIM), jnp.float32)

    def cycle_step(turn_index, cycle_state):
        kv_block, grad_kv, grad_query = cycle_state
        part_query, part_kv = key_block(kv_block, (cycle_index - turn_index) % cycle_size)
        kv_block = from_behind(kv_block, "blk", 1)
        return (kv_block, pass_back(grad_kv + part_kv), grad_query + part_query)

    kv_block, grad_kv, grad_query = lax.fori_loop(
        0, cycle_size - 1, cycle_step, (kv_local, zero_kv, zero_query)
    )
    part_query, part_kv = key_block(kv_block, (cycle_index + 1) % cycle_size)
    grad_kv = pass_back(grad_kv + part_kv)
    grad_query = grad_query + part_query
    grad_qkv = jnp.concatenate(
        [grad_query.reshape(seq_count, pos_count, D), grad_kv], axis=-1
    ).astype(jnp.bfloat16)
    grad_w_qkv = outer_sum(attn_low, grad_qkv)
    grad_in_norm, grad_gain_attn, grad_bias_attn, grad_scale_attn, grad_shift_attn = attn_pull(
        project_back(grad_qkv, w_qkv)
    )
    input_grad = residual_grad + grad_in_norm
    grad_input = input_grad.astype(jnp.bfloat16)
    grad_w_embed = outer_sum(normed_low, grad_input)
    grad_modulation = jnp.concatenate(
        [grad_scale_attn, grad_shift_attn, grad_scale_mlp, grad_shift_mlp], axis=1
    )
    grad_w_time = jnp.dot(
        time_low.astype(jnp.float32).T, grad_modulation, precision=lax.Precision.HIGHEST
    )
    (grad_rows,) = norm_pull(project_back(grad_input, w_embed))
    flat_ids = token_ids.reshape(-1)
    flat_grads = grad_rows.reshape(-1, EMB)
    row_count = VOCAB // lax.axis_size(("dp", "blk"))
    own_start = lax.axis_index(("dp", "blk")) * row_count
    piece_ids = lax.all_gather(flat_ids, ("dp", "blk"), axis=0, tiled=True)
    piece_grads = lax.all_gather(
        flat_grads.astype(jnp.bfloat16), ("dp", "blk"), axis=0, tiled=True
    ).astype(jnp.float32)
    grad_table = scatter_rows(
        jnp.zeros((row_count, EMB), jnp.float32), piece_ids - own_start, piece_grads
    )
    group_count = lax.axis_size("dp")
    gradients = (
        grad_w_embed,
        grad_w_time,
        grad_gain_attn,
        grad_bias_attn,
        grad_gain_mlp,
        grad_bias_mlp,
        grad_w_qkv,
        grad_w_out,
        grad_w_up,
        grad_w_down,
    )
    grouped = tuple((group_columns(g, group_count) for g in gradients))
    in_group = (
        lax.psum_scatter(
            grouped[0].astype(jnp.bfloat16), "blk", scatter_dimension=2, tiled=True
        ).astype(jnp.float32),
        lax.psum_scatter(
            grouped[1].astype(jnp.bfloat16), "blk", scatter_dimension=2, tiled=True
        ).astype(jnp.float32),
        lax.psum_scatter(
            grouped[2].astype(jnp.bfloat16), "blk", scatter_dimension=2, tiled=True
        ).astype(jnp.float32),
        lax.psum_scatter(
            grouped[3].astype(jnp.bfloat16), "blk", scatter_dimension=2, tiled=True
        ).astype(jnp.float32),
        lax.psum_scatter(
            grouped[4].astype(jnp.bfloat16), "blk", scatter_dimension=2, tiled=True
        ).astype(jnp.float32),
        lax.psum_scatter(
            grouped[5].astype(jnp.bfloat16), "blk", scatter_dimension=2, tiled=True
        ).astype(jnp.float32),
        lax.psum_scatter(
            grouped[6].astype(jnp.bfloat16), "blk", scatter_dimension=2, tiled=True
        ).astype(jnp.float32),
        lax.psum_scatter(
            grouped[7].astype(jnp.bfloat16), "blk", scatter_dimension=2, tiled=True
        ).astype(jnp.float32),
        lax.psum_scatter(
            grouped[8].astype(jnp.bfloat16), "blk", scatter_dimension=2, tiled=True
        ).astype(jnp.float32),
        lax.psum_scatter(
            grouped[9].astype(jnp.bfloat16), "blk", scatter_dimension=2, tiled=True
        ).astype(jnp.float32),
    )
    across = (
        lax.psum_scatter(
            in_group[0].astype(jnp.bfloat16), "dp", scatter_dimension=1, tiled=True
        ).astype(jnp.float32),
        lax.psum_scatter(
            in_group[1].astype(jnp.bfloat16), "dp", scatter_dimension=1, tiled=True
        ).astype(jnp.float32),
        lax.psum_scatter(
            in_group[2].astype(jnp.bfloat16), "dp", scatter_dimension=1, tiled=True
        ).astype(jnp.float32),
        lax.psum_scatter(
            in_group[3].astype(jnp.bfloat16), "dp", scatter_dimension=1, tiled=True
        ).astype(jnp.float32),
        lax.psum_scatter(
            in_group[4].astype(jnp.bfloat16), "dp", scatter_dimension=1, tiled=True
        ).astype(jnp.float32),
        lax.psum_scatter(
            in_group[5].astype(jnp.bfloat16), "dp", scatter_dimension=1, tiled=True
        ).astype(jnp.float32),
        lax.psum_scatter(
            in_group[6].astype(jnp.bfloat16), "dp", scatter_dimension=1, tiled=True
        ).astype(jnp.float32),
        lax.psum_scatter(
            in_group[7].astype(jnp.bfloat16), "dp", scatter_dimension=1, tiled=True
        ).astype(jnp.float32),
        lax.psum_scatter(
            in_group[8].astype(jnp.bfloat16), "dp", scatter_dimension=1, tiled=True
        ).astype(jnp.float32),
        lax.psum_scatter(
            in_group[9].astype(jnp.bfloat16), "dp", scatter_dimension=1, tiled=True
        ).astype(jnp.float32),
    )
    summed = tuple(
        (
            a.reshape(g.shape[:-1] + (a.shape[-1],)) if g.ndim == 2 else a.reshape(a.shape[-1])
            for a, g in zip(across, gradients)
        )
    )
    return (
        layer_out,
        grad_input,
        grad_table,
        summed[0],
        summed[1],
        summed[2],
        summed[3],
        summed[4],
        summed[5],
        summed[6],
        summed[7],
        summed[8],
        summed[9],
    )


def solution(mesh):
    return jax.shard_map(
        shards,
        mesh=mesh,
        in_specs=(
            P("dp", "blk"),
            P("dp"),
            P("dp"),
            P(),
            P(),
            P(),
            P(),
            P(),
            P(),
            P(),
            P(),
            P(),
            P(),
            P(),
            P("dp", "blk", None),
        ),
        out_specs=(
            P("dp", "blk", None),
            P("dp", "blk", None),
            P(("dp", "blk"), None),
            P(None, ("dp", "blk")),
            P(None, ("dp", "blk")),
            P(("dp", "blk")),
            P(("dp", "blk")),
            P(("dp", "blk")),
            P(("dp", "blk")),
            P(None, ("dp", "blk")),
            P(None, ("dp", "blk")),
            P(None, ("dp", "blk")),
            P(None, ("dp", "blk")),
        ),
        check_vma=False,
    )
```

profile of v0, /device:TPU:8, one launch (start us, length us, event | category | flops | bytes accessed | tf_op | source)
XLA Modules:
  0.0 1474.0 jit_solution(271567346112141889)
XLA Ops:
  57.5 17.8 %fusion.119 = f32[2,16,512,512]{3,2,1,0:T(8,128)} fusion(bf16[2,512,16,64]{1,3,2,0:T(8,128)(2,1)} %bitcast.229, bf16[2,512,16,64]{1,3,2,0:T(8,128)(2,1)} %bitcast.242), kind=kOutput, calls=%fused_computation.187 | convolution fusion | flops 1073741824 | bytes 37748736 | tf_op jit(solution)/shard_map/while/body/eval_jaxpr/sqhd,skhd->shqk/dot_general | solution.py:123
  87.9 17.8 %fusion.121 = f32[2,16,512,512]{3,2,1,0:T(8,128)} fusion(bf16[2,512,16,64]{1,3,2,0:T(8,128)(2,1)} %bitcast.230, bf16[2,512,16,64]{1,3,2,0:T(8,128)(2,1)} %bitcast.240), kind=kOutput, calls=%fused_computation.189 | convolution fusion | flops 1073741824 | bytes 37748736 | tf_op jit(solution)/shard_map/sqhd,skhd->shqk/dot_general | solution.py:123
  118.0 26.6 %fusion = (f32[2,16,512]{2,1,0:T(8,128)S(1)}, f32[2,16,512,1024]{3,2,1,0:T(8,128)}) fusion(pred[2,1024]{1,0:T(4,128)(4,1)S(1)} %iota_compare_fusion, bf16[2,512,16,64]{1,3,2,0:T(8,128)(2,1)} %bitcast.231, bf16[2,1024,16,64]{1,3,2,0:T(8,128)(2,1)} %bitcast.239), kind=kOutput, calls=%fused_computation.4 | convolution fusion | flops 2197798912 | bytes 73467904 | tf_op jit(solution)/shard_map/sqhd,skhd->shqk/dot_general | solution.py:123
  150.9 21.4 %fusion.1 = f32[2,16,512]{2,1,0:T(8,128)S(1)} fusion(f32[2,16,512,1024]{3,2,1,0:T(8,128)} %get-tuple-element.81, f32[2,16,512]{2,1,0:T(8,128)S(1)} %broadcast_maximum_fusion, pred[2,1024]{1,0:T(4,128)(4,1)S(1)} %iota_compare_fusion), kind=kLoop, calls=%fused_computation.5 | loop fusion | flops 67092480 | bytes 67241984 | tf_op jit(solution)/shard_map/reduce_sum | solution.py:136
  172.4 27.8 %fusion.117 = (bf16[2,512,16,64]{1,3,2,0:T(8,128)(2,1)}, f32[2,512,16,64]{1,3,2,0:T(8,128)}) fusion(f32[2,512,16]{1,2,0:T(8,128)S(1)} %bitcast.273, bf16[2,1024,16,64]{1,3,2,0:T(8,128)(2,1)} %bitcast.263, f32[2,16,512,1024]{3,2,1,0:T(8,128)} %get-tuple-element.81, f32[2,16,512]{2,1,0:T(8,128)S(1)} %broadcast_maximum_fusion, ...), kind=kOutput, calls=%fused_computation.185 | convolution fusion | flops 2216689664 | bytes 77727744 | tf_op jit(solution)/shard_map/shqk,skhd->sqhd/dot_general | solution.py:137
  218.9 24.8 %fusion.16 = bf16[2,512,4096]{2,1,0:T(8,128)(2,1)} fusion(f32[2,512,4096]{2,1,0:T(8,128)} %fusion.26, bf16[4096,1024]{1,0:T(8,128)(2,1)} %param.28, bf16[2,512,1024]{2,1,0:T(8,128)(2,1)} %param.29, f32[2,512]{1,0:T(2,128)S(1)} %get-tuple-element.77), kind=kOutput, calls=%fused_computation.25 | convolution fusion | flops 8676966400 | bytes 35655680 | tf_op jit(solution)/shard_map/dot_general | solution.py:54
  243.6 16.4 %fusion.66 = (bf16[1024]{0:T(1024)(128)(2,1)}, f32[2,1024]{1,0:T(2,128)}, f32[2,512]{1,0:T(2,128)S(1)}, bf16[1024]{0:T(1024)(128)(2,1)}, f32[2,1024]{1,0:T(2,128)}, /*index=5*/f32[2,512,1024]{2,1,0:T(8,128)S(1)}) fusion(f32[2,512]{1,0:T(2,128)S(1)} %fusion.91, f32[2,512,1024]{2,1,0:T(8,128)} %copy-done.9, f32[2,512]{1,0:T(2,128)S(1)} %broadcast_multiply_fusion, ...), kind=kOutput, calls=%fused_computation.88 | convolution fusion | flops 8600413184 | bytes 25206784 | tf_op jit(solution)/shard_map/dot_general | solution.py:54
  275.2 15.9 %fusion.55 = bf16[2,16,64,512]{3,2,1,0:T(8,128)(2,1)} fusion(bf16[2,512,16,64]{1,3,2,0:T(8,128)(2,1)S(1)} %bitcast.251, f32[2,16,512,512]{3,2,1,0:T(8,128)} %fusion.119, f32[2,16,512]{2,1,0:T(8,128)S(1)} %log_add_fusion, pred[2,512]{1,0:T(4,128)(4,1)S(1)} %copy-done.64), kind=kOutput, calls=%fused_computation.79 | convolution fusion | flops 1108344832 | bytes 37815296 | tf_op jit(solution)/shard_map/while/body/eval_jaxpr/shqk,sqhd->skhd/dot_general | solution.py:194
  295.0 22.5 %multiply_convert_fusion.1 = bf16[2,16,512,512]{3,2,1,0:T(8,128)(2,1)} fusion(f32[2,16,512,512]{3,2,1,0:T(8,128)} %fusion.119, bf16[2,512,16,64]{1,3,2,0:T(8,128)(2,1)} %bitcast.252, bf16[2,512,16,64]{1,3,2,0:T(8,128)(2,1)} %bitcast.266, f32[2,16,512]{2,1,0:T(8,128)S(1)} %bitcast.278, f32[2,16,512]{2,1,0:T(8,128)S(1)} %log_add_fusion, ...), kind=kOutput, calls=%fused_computation.11 | convolution fusion | flops 1132462080 | bytes 54658048 | tf_op jit(solution)/shard_map/while/body/eval_jaxpr/sqhd,skhd->shqk/dot_general | solution.py:182
  336.8 16.9 %fusion.17 = f32[2,16,64,512]{3,2,1,0:T(8,128)} fusion(bf16[2,512,16,64]{1,3,2,0:T(8,128)(2,1)} %bitcast.253, f32[2,16,512,512]{3,2,1,0:T(8,128)} %fusion.121, f32[2,16,512]{2,1,0:T(8,128)S(1)} %log_add_fusion, pred[2,512]{1,0:T(4,128)(4,1)S(1)} %copy-done.63), kind=kOutput, calls=%fused_computation.29 | convolution fusion | flops 1107296256 | bytes 39912448 | tf_op jit(solution)/shard_map/shqk,sqhd->skhd/dot_general | solution.py:194
  359.0 22.4 %multiply_convert_fusion = bf16[2,16,512,512]{3,2,1,0:T(8,128)(2,1)} fusion(f32[2,16,512,512]{3,2,1,0:T(8,128)} %fusion.121, bf16[2,512,16,64]{1,3,2,0:T(8,128)(2,1)} %bitcast.254, bf16[2,512,16,64]{1,3,2,0:T(8,128)(2,1)} %bitcast.267, f32[2,16,512]{2,1,0:T(8,128)S(1)} %bitcast.279, f32[2,16,512]{2,1,0:T(8,128)S(1)} %log_add_fusion, ...), kind=kOutput, calls=%fused_computation.9 | convolution fusion | flops 1132462080 | bytes 54658048 | tf_op jit(solution)/shard_map/sqhd,skhd->shqk/dot_general | solution.py:182
  473.3 15.4 %bitcast_convert_fusion.1 = bf16[1024,4096]{1,0:T(8,128)(2,1)} fusion(bf16[2,512,4096]{2,1,0:T(8,128)(2,1)} %fusion.16, f32[2,512,1024]{2,1,0:T(8,128)} %copy-done.9, f32[2,1024]{1,0:T(2,128)S(1)} %copy-done.52, f32[2,1024]{1,0:T(2,128)S(1)} %copy-done.43, f32[2,512]{1,0:T(2,128)S(1)} %copy-done.45, f32[2,512]{1,0:T(2,128)S(1)} %copy-done.33), kind=kOutput, calls=%fused_computation.27 | convolution fusion | flops 8599371776 | bytes 20996096 | tf_op jit(solution)/shard_map/dot_general | solution.py:63
  512.1 15.7 %copy.148 = bf16[32,8,16,1024]{3,1,2,0:T(8,128)(2,1)} copy(bf16[32,8,16,1024]{3,2,1,0:T(8,128)(2,1)} %bitcast.236) | data formatting | bytes 16777216
  527.8 16.4 %bitcast_convert_fusion = bf16[4096,1024]{0,1:T(8,128)(2,1)} fusion(bf16[2,512,1024]{2,1,0:T(8,128)(2,1)} %param.29, f32[2,512]{1,0:T(2,128)S(1)} %copy-done.39, f32[2,512,4096]{2,1,0:T(8,128)} %fusion.26), kind=kOutput, calls=%fused_computation.26 | convolution fusion | flops 8635023360 | bytes 27267072 | tf_op jit(solution)/shard_map/dot_general | solution.py:63
  595.6 35.5 %all_gather.10 = s32[32768]{0:T(1024)S(1)} all-gather(s32[1024]{0:T(1024)S(1)} %bitcast.284), channel_id=1, replica_groups=mesh['dp'=16,'blk'=2] {'dp','blk'}, dimensions={0}, use_global_device_ids=true | all-gather | bytes 135168 | tf_op jit(solution)/shard_map/all_gather | solution.py:248
  631.1 17.8 %multiply_convert_fusion.3 = bf16[2,512,1024]{2,1,0:T(8,128)(2,1)} fusion(f32[2,512,1024]{2,1,0:T(8,128)} %copy-done.9, bf16[4096,1024]{1,0:T(8,128)(2,1)} %param.28, f32[2,512]{1,0:T(2,128)S(1)} %copy-done.39, f32[2,512,4096]{2,1,0:T(8,128)} %fusion.26), kind=kOutput, calls=%fused_computation.64 | convolution fusion | flops 8630829056 | bytes 31461376 | tf_op jit(solution)/shard_map/dot_general | solution.py:45
  650.5 31.4 %reduce-scatter.45.cloned.1.call-done = bf16[1024,1,32]{0,2,1:T(8,128)(2,1)} async-done(((bf16[1024,16,32]{0,2,1:T(8,128)(2,1)}), bf16[1024,1,32]{0,2,1:T(8,128)(2,1)}) %reduce-scatter.45.cloned.1.call-update) | async-done | bytes 65552 | tf_op jit(solution)/shard_map/reduce_scatter | solution.py:323
  707.3 71.0 %all-reduce.4 = (bf16[1,16,32]{2,1,0:T(8,128)(2,1)S(1)}, bf16[1,16,32]{2,1,0:T(8,128)(2,1)S(1)}, bf16[1,16,32]{2,1,0:T(8,128)(2,1)S(1)}, bf16[1,16,32]{2,1,0:T(8,128)(2,1)S(1)}) all-reduce(bf16[1,16,32]{2,1,0:T(8,128)(2,1)S(1)} %copy.119, bf16[1,16,32]{2,1,0:T(8,128)(2,1)S(1)} %copy.123, ...), channel_id=7, replica_groups=mesh['dp'=16,'blk'=2] {'dp'}, use_global_device_ids=true, to_apply=%region_24.25.clone | all-reduce | flops 2048 | bytes 8192
  784.2 71.5 %reduce-scatter.37.cloned.1.call-done = bf16[256,1,128]{2,0,1:T(8,128)(2,1)} async-done(((bf16[256,16,128]{2,0,1:T(8,128)(2,1)}), bf16[256,1,128]{2,0,1:T(8,128)(2,1)}) %reduce-scatter.37.cloned.1.call-update) | async-done | bytes 65552 | tf_op jit(solution)/shard_map/reduce_scatter | solution.py:305
  857.3 96.9 %reduce-scatter.47.cloned.1.call-done = bf16[1024,1,128]{2,0,1:T(8,128)(2,1)} async-done(((bf16[1024,16,128]{2,0,1:T(8,128)(2,1)}), bf16[1024,1,128]{2,0,1:T(8,128)(2,1)}) %reduce-scatter.47.cloned.1.call-update) | async-done | bytes 262160 | tf_op jit(solution)/shard_map/reduce_scatter | solution.py:326
  955.9 95.2 %reduce-scatter.51.cloned.1.call-done = bf16[4096,1,32]{0,2,1:T(8,128)(2,1)} async-done(((bf16[4096,16,32]{0,2,1:T(8,128)(2,1)}), bf16[4096,1,32]{0,2,1:T(8,128)(2,1)}) %reduce-scatter.51.cloned.1.call-update) | async-done | bytes 262160 | tf_op jit(solution)/shard_map/reduce_scatter | solution.py:329
  1052.9 135.8 %reduce-scatter.41.cloned.1.call-done = bf16[1024,1,96]{0,2,1:T(8,128)(2,1)} async-done(((bf16[1024,16,96]{0,2,1:T(8,128)(2,1)}), bf16[1024,1,96]{0,2,1:T(8,128)(2,1)}) %reduce-scatter.41.cloned.1.call-update) | async-done | bytes 196624 | tf_op jit(solution)/shard_map/reduce_scatter | solution.py:320
  1190.4 115.1 %all-gather.5.cloned.1.call-done = bf16[32768,256]{1,0:T(8,128)(2,1)} async-done(((bf16[1024,256]{1,0:T(8,128)(2,1)}), bf16[32768,256]{1,0:T(8,128)(2,1)}) %all-gather.5.cloned.1.call-update) | async-done | bytes 16777232 | tf_op jit(solution)/shard_map/all_gather | solution.py:249
  1305.5 161.2 %scatter_custom_fusion = f32[1000,256]{1,0:T(8,128)} fusion(s32[32768]{0:T(1024)S(1)} %compare_select_fusion, bf16[32768,256]{1,0:T(8,128)(2,1)} %all-gather.5.cloned.1.call-done, f32[]{:T(128)} %constant.35.clone.1), kind=kCustom, calls=%fused_computation.7 | custom fusion | flops 16777216 | bytes 17801220 | tf_op jit(solution)/shard_map/scatter-add | solution.py:71
  (312 shorter events, 349.0 us)
Async XLA Ops:
  7.2 193.0 %copy-start = (bf16[1024,1024]{1,0:T(8,128)(2,1)S(1)}, bf16[1024,1024]{1,0:T(8,128)(2,1)}, u32[]{:S(2)}) copy-start(bf16[1024,1024]{1,0:T(8,128)(2,1)} %param.26) | copy-start | bytes 6291460
  7.2 98.5 %all-gather.3.cloned.1.call-start = ((), (), s32[]{:S(2)}) async-start(), calls=%async_computation.16 | async-start | bytes 12582912 | tf_op jit(solution)/shard_map/all_gather | solution.py:128
  22.4 237.7 %copy-start.42 = (f32[2,1024]{1,0:T(2,128)}, f32[2,1024]{1,0:T(2,128)S(1)}, u32[]{:S(2)}) copy-start(f32[2,1024]{1,0:T(2,128)S(1)} %get-tuple-element.69) | copy-start | bytes 24580
  38.2 531.4 %reduce-scatter.43.cloned.1.call-start = ((), (), s32[]{:S(2)}) async-start(), calls=%async_computation.23 | async-start | bytes 3145728 | tf_op jit(solution)/shard_map/reduce_scatter | solution.py:291
  38.5 36.8 %collective-permute-start = (bf16[2,512,2048]{2,1,0:T(8,128)(2,1)}, bf16[2,512,2048]{2,1,0:T(8,128)(2,1)}, u32[]{:S(2)}, u32[]{:S(2)}) collective-permute-start(bf16[2,512,2048]{2,1,0:T(8,128)(2,1)} %slice.38), channel_id=1, source_target_pairs={{0,1},{1,0},{2,3},{3,2},{4,5},{5,4},{6,7},{7,6},{8,9},{9,8},{10,11... | collective-permute-start | bytes 12582920 | tf_op jit(solution)/shard_map/while/body/eval_jaxpr/ppermute | solution.py:22
  57.5 204.1 %copy-start.38 = (f32[2,512]{1,0:T(2,128)}, f32[2,512]{1,0:T(2,128)S(1)}, u32[]{:S(2)}) copy-start(f32[2,512]{1,0:T(2,128)S(1)} %get-tuple-element.77) | copy-start | bytes 12292
  336.2 64.0 %collective-permute-start.1 = (bf16[2,512,2048]{2,1,0:T(8,128)(2,1)}, bf16[2,512,2048]{2,1,0:T(8,128)(2,1)}, u32[]{:S(2)}, u32[]{:S(2)}) collective-permute-start(bf16[2,512,2048]{2,1,0:T(8,128)(2,1)} %pad_maximum_fusion.1), channel_id=1, source_target_pairs={{0,1},{1,0},{2,3},{3,2},{4,5},{5,4},{6,7},{7,6},{8,9},{9,8},{10,11... | collective-permute-start | bytes 12582920 | tf_op jit(solution)/shard_map/while/body/eval_jaxpr/ppermute | solution.py:22
  407.2 32.3 %collective-permute-start.2 = (bf16[2,512,2048]{2,1,0:T(8,128)(2,1)}, bf16[2,512,2048]{2,1,0:T(8,128)(2,1)}, u32[]{:S(2)}, u32[]{:S(2)}) collective-permute-start(bf16[2,512,2048]{2,1,0:T(8,128)(2,1)} %fusion.23), channel_id=1, source_target_pairs={{0,1},{1,0},{2,3},{3,2},{4,5},{5,4},{6,7},{7,6},{8,9},{9,8},{10,11... | collective-permute-start | bytes 12582920 | tf_op jit(solution)/shard_map/ppermute | solution.py:22
  411.0 160.9 %reduce-scatter.33.cloned.1.call-start = ((), (), s32[]{:S(2)}) async-start(), calls=%async_computation.18 | async-start | bytes 786432 | tf_op jit(solution)/shard_map/reduce_scatter | solution.py:270
  460.0 112.7 %reduce-scatter.53.cloned.1.call-start = ((), (), s32[]{:S(2)}) async-start(), calls=%async_computation.28 | async-start | bytes 3145728
  473.2 103.1 %reduce-scatter.63.cloned.1.call-start = ((), (), s32[]{:S(2)}) async-start(), calls=%async_computation.33 | async-start | bytes 12582912
  527.8 62.3 %reduce-scatter.49.cloned.1.call-start = ((), (), s32[]{:S(2)}) async-start(), calls=%async_computation.26 | async-start | bytes 12582912 | tf_op jit(solution)/shard_map/reduce_scatter | solution.py:297
  544.3 46.4 %reduce-scatter.39.cloned.1.call-start = ((), (), s32[]{:S(2)}) async-start(), calls=%async_computation.21 | async-start | bytes 9437184 | tf_op jit(solution)/shard_map/reduce_scatter | solution.py:288
  567.2 81.7 %reduce-scatter.59.cloned.1.call-start = ((), (), s32[]{:S(2)}) async-start(), calls=%async_computation.31 | async-start | bytes 24576
  568.7 81.0 %reduce-scatter.61.cloned.1.call-start = ((), (), s32[]{:S(2)}) async-start(), calls=%async_computation.32 | async-start | bytes 24576
  569.6 112.3 %reduce-scatter.45.cloned.1.call-start = ((), (), s32[]{:S(2)}) async-start(), calls=%async_computation.24 | async-start | bytes 1114112 | tf_op jit(solution)/shard_map/reduce_scatter | solution.py:323
  570.1 125.1 %reduce-scatter.55.cloned.1.call-start = ((), (), s32[]{:S(2)}) async-start(), calls=%async_computation.29 | async-start | bytes 24576
  571.0 135.5 %reduce-scatter.57.cloned.1.call-start = ((), (), s32[]{:S(2)}) async-start(), calls=%async_computation.30 | async-start | bytes 24576
  571.9 211.0 %reduce-scatter.35.cloned.1.call-start = ((), (), s32[]{:S(2)}) async-start(), calls=%async_computation.19 | async-start | bytes 278528 | tf_op jit(solution)/shard_map/reduce_scatter | solution.py:302
  572.6 283.1 %reduce-scatter.37.cloned.1.call-start = ((), (), s32[]{:S(2)}) async-start(), calls=%async_computation.20 | async-start | bytes 1114112 | tf_op jit(solution)/shard_map/reduce_scatter | solution.py:305
  575.9 378.2 %reduce-scatter.47.cloned.1.call-start = ((), (), s32[]{:S(2)}) async-start(), calls=%async_computation.25 | async-start | bytes 4456448 | tf_op jit(solution)/shard_map/reduce_scatter | solution.py:326
  590.0 461.1 %reduce-scatter.51.cloned.1.call-start = ((), (), s32[]{:S(2)}) async-start(), calls=%async_computation.27 | async-start | bytes 4456448 | tf_op jit(solution)/shard_map/reduce_scatter | solution.py:329
  590.6 598.1 %reduce-scatter.41.cloned.1.call-start = ((), (), s32[]{:S(2)}) async-start(), calls=%async_computation.22 | async-start | bytes 3342336 | tf_op jit(solution)/shard_map/reduce_scatter | solution.py:320
  591.3 714.2 %all-gather.5.cloned.1.call-start = ((), (), s32[]{:S(2)}) async-start(), calls=%async_computation.17 | async-start | bytes 17301504 | tf_op jit(solution)/shard_map/all_gather | solution.py:249
  (69 other events, 811.8 us)
Sparse Core Ops, SparseCore 0:
  38.3 21.2 all-gather.2
  411.1 11.2 reduce-scatter.42
  460.2 9.5 reduce-scatter.32
  473.3 11.2 reduce-scatter.52
  527.9 18.4 reduce-scatter.62
  548.6 18.0 reduce-scatter.48
  569.1 15.6 reduce-scatter.38
  587.5 8.5 reduce-scatter.58
  598.9 8.5 reduce-scatter.60
  609.6 72.2 reduce-scatter.44
  684.7 10.4 reduce-scatter.54
  697.9 8.5 reduce-scatter.56
  708.8 70.7 reduce-scatter.34
  781.7 73.9 reduce-scatter.36
  858.0 96.0 reduce-scatter.46
  956.4 94.7 reduce-scatter.50
  1056.7 131.9 reduce-scatter.40
  1192.4 113.0 all-gather.4
where the time goes:
time: 1480 us; the launch traced here: 1470 us
  waiting for transfers between devices  571 us (39%)
  matrix products  369 us (25%)
  other arithmetic  223 us (15%)
  local copies, waits for them, and re-layouts  187 us (13%)
  blocking collectives  106 us (7%)
  between operations  15.9 us (1%)
    scatter-add x1, other arithmetic, scatter_rows(): running_total.at[jnp.where(inside, offsets, row_span)]  161 us
    reduce_scatter x1, waiting for transfers between devices, shards(): lax.psum_scatter(in_group[6].astype(jnp.bfloat16), 'dp', scatter_dimensio...  136 us
    all_gather x1, waiting for transfers between devices, shards(): lax.all_gather(flat_grads.astype(jnp.bfloat16), ('dp', 'blk'), axis=0, ti...  115 us
    reduce_scatter x1, waiting for transfers between devices, shards(): lax.psum_scatter(in_group[8].astype(jnp.bfloat16), 'dp', scatter_dimensio...  96.9 us
    reduce_scatter x1, waiting for transfers between devices, shards(): lax.psum_scatter(in_group[9].astype(jnp.bfloat16), 'dp', scatter_dimensio...  95.2 us
    unnamed x173, local copies, waits for them, and re-layouts  86.1 us
    reduce_scatter x1, waiting for transfers between devices, shards(): lax.psum_scatter(in_group[1].astype(jnp.bfloat16), 'dp', scatter_dimensio...  71.5 us
    unnamed x1, blocking collectives  71 us
  transfers between devices with their start and end apart: 21, of which 8 were waited for; matrix products, arithmetic and copies ran while one was open for 23% of the time, Pallas kernels for 0%

commit v1 on v0

--- a/solution.py
+++ b/solution.py
@@ -1,8 +1,11 @@
+import functools
 import math
 
 import jax
 import jax.numpy as jnp
 from jax import lax
+from jax.experimental import pallas as pl
+from jax.experimental.pallas import tpu as pltpu
 from jax.sharding import PartitionSpec as P
 
 D = 1024
@@ -77,7 +80,7 @@
     return matrix.reshape(matrix.shape[0], group_count, matrix.shape[1] // group_count)
 
 
-def shards(
+def split_position_shards(
     token_ids,
     seq_lengths,
     diffusion_time,
@@ -351,6 +354,842 @@
         summed[8],
         summed[9],
     )
+
+
+BF16 = jnp.bfloat16
+F32 = jnp.float32
+LOG2_E = 1.4426950408889634
+VMEM_BYTES = 58 * 1024 * 1024
+META_ROWS = 4
+SLOT_ROWS = 72
+EXACT_BASE = 256
+TOKEN_TILE = 256
+ANY_SPEC = pl.BlockSpec(memory_space=pl.ANY)
+
+
+def dot_nn(left, right):
+    return lax.dot_general(left, right, (((1,), (0,)), ((), ())), preferred_element_type=F32)
+
+
+def dot_nt(left, right):
+    return lax.dot_general(left, right, (((1,), (1,)), ((), ())), preferred_element_type=F32)
+
+
+def dot_tn(left, right):
+    return lax.dot_general(left, right, (((0,), (0,)), ((), ())), preferred_element_type=F32)
+
+
+def head_operands(queries, keys, head, length):
+    lane = lax.broadcasted_iota(jnp.int32, queries.shape, 1)
+    row = lax.broadcasted_iota(jnp.int32, queries.shape, 0)
+    mine = (lane // HEAD_DIM) == head
+    spare = lane == (1 - head) * HEAD_DIM
+    zero = jnp.zeros_like(queries)
+    fill = jnp.where(row >= length, jnp.full_like(queries, NEG_FILL), zero)
+    one_query = jnp.where(mine, queries, jnp.where(spare, jnp.ones_like(queries), zero))
+    one_key = jnp.where(mine, keys, jnp.where(spare, fill, zero))
+    return mine, one_query, one_key
+
+
+def attend_kernel(length_ref, q_ref, k_ref, v_ref, out_ref, lse_ref):
+    length = length_ref[0]
+    factor = LOG2_E * HEAD_DIM**-0.5
+    rows = []
+    for head in range(2):
+        mine, one_query, one_key = head_operands(q_ref[...], k_ref[...], head, length)
+        value_one = jnp.where(mine, v_ref[...], jnp.ones_like(v_ref[...]))
+        scores = dot_nt(one_key, one_query)
+        top = jnp.max(scores, axis=0, keepdims=True)
+        weights = jnp.exp2(scores * factor - top * factor).astype(BF16)
+        mixed = dot_tn(value_one, weights)
+        other = (1 - head) * HEAD_DIM
+        total = mixed[other : other + 1]
+        lse_ref[0, head : head + 1, :] = top * factor + jnp.log2(total)
+        rows.append(mixed[head * HEAD_DIM : (head + 1) * HEAD_DIM] * (1.0 / total))
+    out_ref[...] = jnp.transpose(jnp.concatenate(rows, axis=0), (1, 0)).astype(BF16)
+
+
+def attend_back_kernel(
+    length_ref, q_ref, k_ref, v_ref, out_ref, grad_ref, lse_ref, dq_ref, dk_ref, dv_ref, *, chunk
+):
+    length = length_ref[0]
+    positions = q_ref.shape[0]
+    factor = LOG2_E * HEAD_DIM**-0.5
+    scale = HEAD_DIM**-0.5
+    grad = grad_ref[...]
+    product = grad.astype(F32) * out_ref[...].astype(F32)
+    high = product.astype(BF16)
+    low = (product - high.astype(F32)).astype(BF16)
+    head_of_lane = lax.broadcasted_iota(jnp.int32, (16, 2 * HEAD_DIM), 1) // HEAD_DIM
+    picker = jnp.where(
+        head_of_lane == lax.broadcasted_iota(jnp.int32, (16, 2 * HEAD_DIM), 0), 1.0, 0.0
+    ).astype(BF16)
+    delta = dot_nt(picker, high) + dot_nt(picker, low)
+    query_rows = []
+    key_parts = ([], [])
+    value_parts = ([], [])
+    for head in range(2):
+        mine, one_query, one_key = head_operands(q_ref[...], k_ref[...], head, length)
+        one_value = jnp.where(mine, v_ref[...], jnp.zeros_like(v_ref[...]))
+        lse = lse_ref[0, head : head + 1, :]
+        row_delta = delta[head : head + 1, :]
+        query_grad = jnp.zeros((2 * HEAD_DIM, positions), F32)
+        for start in range(0, positions, chunk):
+            span = slice(start, start + chunk)
+            weights = jnp.exp2(dot_nt(one_key[span], one_query) * factor - lse)
+            weight_grad = dot_nt(one_value[span], grad)
+            score_grad = (weights * (weight_grad - row_delta)).astype(BF16)
+            value_parts[head].append(dot_nn(weights.astype(BF16), grad))
+            key_parts[head].append(dot_nn(score_grad, q_ref[...]))
+            query_grad = query_grad + dot_tn(k_ref[span, :], score_grad)
+        query_rows.append(query_grad[head * HEAD_DIM : (head + 1) * HEAD_DIM])
+    first = lax.broadcasted_iota(jnp.int32, (chunk, 2 * HEAD_DIM), 1) < HEAD_DIM
+    for part, start in enumerate(range(0, positions, chunk)):
+        span = slice(start, start + chunk)
+        dk_ref[span, :] = (jnp.where(first, key_parts[0][part], key_parts[1][part]) * scale).astype(BF16)
+        dv_ref[span, :] = jnp.where(first, value_parts[0][part], value_parts[1][part]).astype(BF16)
+    dq_ref[...] = jnp.transpose(jnp.concatenate(query_rows, axis=0) * scale, (1, 0)).astype(BF16)
+
+
+def gelu_with_slope(values):
+    root = math.sqrt(2.0 / math.pi)
+    square = values * values
+    bend = jnp.tanh(root * values * (1.0 + 0.044715 * square))
+    half = 0.5 * (1.0 + bend)
+    slope = half + 0.5 * values * (1.0 - bend * bend) * (root * (1.0 + 3.0 * 0.044715 * square))
+    return values * half, slope
+
+
+def swap_core(value):
+    return lax.ppermute(value, "blk", [(0, 1), (1, 0)])
+
+
+def join_halves(core, own, other):
+    first = jnp.where(core == 0, own, other)
+    second = jnp.where(core == 0, other, own)
+    return jnp.concatenate([first, second], axis=0)
+
+
+def to_whole(core, local):
+    own = lax.dynamic_index_in_dim(local, core, 0, keepdims=False)
+    away = lax.dynamic_index_in_dim(local, 1 - core, 0, keepdims=False)
+    return join_halves(core, own, swap_core(away))
+
+
+def to_split(core, whole):
+    half = whole.shape[0] // 2
+    halves = whole.reshape((2, half) + whole.shape[1:])
+    own = lax.dynamic_index_in_dim(halves, core, 0, keepdims=False)
+    away = swap_core(lax.dynamic_index_in_dim(halves, 1 - core, 0, keepdims=False))
+    return jnp.stack([jnp.where(core == 0, own, away), jnp.where(core == 0, away, own)])
+
+
+COST_SHARE = 0.3
+
+
+def kernel_cost(microseconds):
+    flops = int(COST_SHARE * microseconds * 1e9)
+    return pl.CostEstimate(flops=flops, bytes_accessed=1024, transcendentals=0)
+
+
+def run_kernel(
+    body, grid, scalars, inputs, in_specs, out_specs, out_shape, microseconds, name, scratch=(), carried=()
+):
+    scalar_count, input_count, output_count = len(scalars), len(inputs), len(out_shape)
+    carried_count = len(carried)
+    first_carried = scalar_count + input_count
+
+    def kernel(*refs):
+        rest = refs[first_carried + carried_count :]
+        body(*refs[:first_carried], *rest[:output_count], *rest[output_count + carried_count :])
+
+    results = pl.pallas_call(
+        kernel,
+        grid_spec=pltpu.PrefetchScalarGridSpec(
+            num_scalar_prefetch=scalar_count,
+            grid=grid,
+            in_specs=list(in_specs) + [ANY_SPEC] * carried_count,
+            out_specs=list(out_specs) + [ANY_SPEC] * carried_count,
+            scratch_shapes=list(scratch),
+        ),
+        out_shape=list(out_shape) + [jax.ShapeDtypeStruct(c.shape, c.dtype) for c in carried],
+        input_output_aliases={first_carried + i: output_count + i for i in range(carried_count)},
+        compiler_params=pltpu.CompilerParams(vmem_limit_bytes=VMEM_BYTES),
+        cost_estimate=kernel_cost(microseconds),
+        name=name,
+    )(*scalars, *inputs, *carried)
+    return results[:output_count], results[output_count:]
+
+
+def behind(*arrays):
+    def kernel(*refs):
+        pass
+
+    return pl.pallas_call(
+        kernel,
+        in_specs=[ANY_SPEC] * len(arrays),
+        out_specs=[ANY_SPEC] * len(arrays),
+        out_shape=[jax.ShapeDtypeStruct(a.shape, a.dtype) for a in arrays],
+        input_output_aliases={i: i for i in range(len(arrays))},
+        compiler_params=pltpu.CompilerParams(vmem_limit_bytes=VMEM_BYTES),
+        cost_estimate=kernel_cost(1),
+        name="behind",
+    )(*arrays)
+
+
+def shaped(dtype, *shape):
+    return jax.ShapeDtypeStruct(shape, dtype)
+
+
+def row_spec(tile, columns):
+    return pl.BlockSpec((tile, columns), lambda i, *scalars: (i, 0))
+
+
+def fixed_spec(*shape):
+    return pl.BlockSpec(shape, lambda *grid: (0,) * len(shape))
+
+
+def attend(length, qkv):
+    positions = qkv.shape[0]
+    pairs = HEADS // 2
+
+    def spec(group):
+        return pl.BlockSpec((positions, 2 * HEAD_DIM), lambda pair, length: (0, group * pairs + pair))
+
+    results, _ = run_kernel(
+        attend_kernel,
+        (pairs,),
+        [length],
+        [qkv, qkv, qkv],
+        [spec(0), spec(1), spec(2)],
+        [spec(0), pl.BlockSpec((1, 2, positions), lambda pair, length: (pair, 0, 0))],
+        [shaped(BF16, positions, D), shaped(F32, pairs, 2, positions)],
+        30,
+        "attend",
+    )
+    return results
+
+
+def attend_back(length, qkv, attended, grad_att, lse, part, parts, grads, carried):
+    positions = qkv.shape[0]
+    pairs = HEADS // 2
+    count = pairs // parts
+    shift = part * count
+
+    def spec(group):
+        return pl.BlockSpec(
+            (positions, 2 * HEAD_DIM), lambda pair, length: (0, group * pairs + shift + pair)
+        )
+
+    lse_spec = pl.BlockSpec((1, 2, positions), lambda pair, length: (shift + pair, 0, 0))
+    inputs = [qkv, qkv, qkv, attended, grad_att, lse]
+    held = len(grads)
+    kept = len(carried)
+
+    def kernel(*refs):
+        attend_back_kernel(*refs[:7], *refs[7 + held + kept : 10 + held + kept], chunk=min(512, positions))
+
+    aliases = {7 + i: i for i in range(held)}
+    aliases.update({7 + held + i: 3 + i for i in range(kept)})
+    results = pl.pallas_call(
+        kernel,
+        grid_spec=pltpu.PrefetchScalarGridSpec(
+            num_scalar_prefetch=1,
+            grid=(count,),
+            in_specs=[spec(0), spec(1), spec(2), spec(0), spec(0), lse_spec] + [ANY_SPEC] * (held + kept),
+            out_specs=[spec(0)] * 3 + [ANY_SPEC] * kept,
+        ),
+        out_shape=[shaped(BF16, positions, D)] * 3 + [jax.ShapeDtypeStruct(c.shape, c.dtype) for c in carried],
+        input_output_aliases=aliases,
+        compiler_params=pltpu.CompilerParams(vmem_limit_bytes=VMEM_BYTES),
+        cost_estimate=kernel_cost(46 / parts),
+        name="attend_back",
+    )(length, *inputs, *grads, *carried)
+    return results[:3], results[3:]
+
+
+def norm_rows(features):
+    center = features - jnp.mean(features, axis=-1, keepdims=True)
+    rstd = lax.rsqrt(jnp.mean(center * center, axis=-1, keepdims=True) + 1e-05)
+    return center * rstd, rstd
+
+
+def norm_rows_back(grad_norm, xhat, rstd, gain_row):
+    scaled = grad_norm * gain_row
+    mean_scaled = jnp.mean(scaled, axis=-1, keepdims=True)
+    mean_cross = jnp.mean(scaled * xhat, axis=-1, keepdims=True)
+    return rstd * (scaled - mean_scaled - xhat * mean_cross)
+
+
+def add_column_sums(sums_ref, grad_norm, xhat):
+    sums_ref[0:1, :] += jnp.sum(grad_norm * xhat, axis=0, keepdims=True)
+    sums_ref[1:2, :] += jnp.sum(grad_norm, axis=0, keepdims=True)
+
+
+def valid_column(length, tile):
+    row = lax.broadcasted_iota(jnp.int32, (tile, 1), 0) + pl.program_id(0) * tile
+    return row < length
+
+
+def share_out(core, value, keep_ref, away_ref):
+    rows = keep_ref.shape[-2]
+    if len(keep_ref.shape) == 4:
+        outer, inner = keep_ref.shape[:2]
+        value = value.astype(BF16).reshape(outer, inner, 2, rows, value.shape[1])
+        first, second = value[:, :, 0], value[:, :, 1]
+        keep_ref[...] = jnp.where(core == 0, first, second)
+        away_ref[...] = jnp.where(core == 0, second, first)
+        return
+    groups = keep_ref.shape[0]
+    value = value.astype(BF16).reshape(groups, 2, rows, value.shape[1])
+    first, second = value[:, 0], value[:, 1]
+    keep_ref[...] = jnp.where(core == 0, first, second)
+    away_ref[...] = jnp.where(core == 0, second, first)
+
+
+def embed_kernel(emb_ref, we_ref, gain_ref, shift_ref, wqkv_ref, low_ref, in_ref, attn_ref, qkv_ref):
+    rows = emb_ref[...].astype(F32)
+    normed = rows * lax.rsqrt(jnp.mean(rows * rows, axis=-1, keepdims=True) + 1e-06)
+    low = normed.astype(BF16)
+    low_ref[...] = low
+    inputs = dot_nn(low, we_ref[...])
+    in_ref[...] = inputs
+    xhat, _ = norm_rows(inputs)
+    attn = (xhat * gain_ref[...] + shift_ref[...]).astype(BF16)
+    attn_ref[...] = attn
+    qkv_ref[...] = dot_nn(attn, wqkv_ref[...]).astype(BF16)
+
+
+def embed_and_project(emb, w_embed, gain_row, shift_row, w_qkv):
+    count = emb.shape[0]
+    tile = TOKEN_TILE
+    results, _ = run_kernel(
+        embed_kernel,
+        (count // tile,),
+        [],
+        [emb, w_embed, gain_row, shift_row, w_qkv],
+        [row_spec(tile, EMB), fixed_spec(EMB, D), fixed_spec(1, D), fixed_spec(1, D), fixed_spec(D, 3 * D)],
+        [row_spec(tile, EMB), row_spec(tile, D), row_spec(tile, D), row_spec(tile, 3 * D)],
+        [shaped(BF16, count, EMB), shaped(F32, count, D), shaped(BF16, count, D), shaped(BF16, count, 3 * D)],
+        12,
+        "embed_and_project",
+    )
+    return results
+
+
+def residual_kernel(length_ref, att_ref, in_ref, wo_ref, gain_ref, shift_ref, cot_ref, res_ref, mlp_ref, fin_ref):
+    residual = in_ref[...] + dot_nn(att_ref[...], wo_ref[...])
+    res_ref[...] = residual
+    xhat, _ = norm_rows(residual)
+    mlp_ref[...] = (xhat * gain_ref[...] + shift_ref[...]).astype(BF16)
+    cot = cot_ref[...]
+    fin_ref[...] = jnp.where(valid_column(length_ref[0], cot.shape[0]), cot, jnp.zeros_like(cot))
+
+
+def attention_residual(length, attended, inputs, w_out, gain_row, shift_row, cot):
+    count = attended.shape[0]
+    row = row_spec(TOKEN_TILE, D)
+    results, _ = run_kernel(
+        residual_kernel,
+        (count // TOKEN_TILE,),
+        [length],
+        [attended, inputs, w_out, gain_row, shift_row, cot],
+        [row, row, fixed_spec(D, D), fixed_spec(1, D), fixed_spec(1, D), row],
+        [row, row, row],
+        [shaped(F32, count, D), shaped(BF16, count, D), shaped(BF16, count, D)],
+        8,
+        "attention_residual",
+    )
+    return results
+
+
+def feed_forward_kernel(
+    core_ref, mlp_ref, fin_ref, wu_ref, wd_ref, down_in_ref, grad_in_ref,
+    gwd_keep_ref, gwd_away_ref, gwu_keep_ref, gwu_away_ref, down_ref, grad_ref,
+    fin_t_ref, hid_ref, pre_ref, *, first
+):
+    core = core_ref[0]
+    count = mlp_ref.shape[0]
+
+    @pl.when(pl.program_id(0) == 0)
+    def _():
+        fin_t_ref[...] = jnp.transpose(fin_ref[...], (1, 0))
+        if first:
+            down_ref[...] = jnp.zeros_like(down_ref)
+            grad_ref[...] = jnp.zeros_like(grad_ref)
+        else:
+            down_ref[...] = down_in_ref[...]
+            grad_ref[...] = grad_in_ref[...]
+
+    for start in range(0, count, TOKEN_TILE):
+        span = slice(start, start + TOKEN_TILE)
+        hidden, slope = gelu_with_slope(dot_nn(mlp_ref[span, :], wu_ref[...]))
+        hid_ref[span, :] = hidden.astype(BF16)
+        pre_ref[span, :] = (dot_nt(fin_ref[span, :], wd_ref[...]) * slope).astype(BF16)
+    share_out(core, dot_nn(fin_t_ref[...], hid_ref[...]), gwd_keep_ref, gwd_away_ref)
+    share_out(core, dot_tn(pre_ref[...], mlp_ref[...]), gwu_keep_ref, gwu_away_ref)
+    for start in range(0, count, TOKEN_TILE):
+        span = slice(start, start + TOKEN_TILE)
+        down_ref[span, :] += dot_nn(hid_ref[span, :], wd_ref[...])
+        grad_ref[span, :] += dot_nt(pre_ref[span, :], wu_ref[...])
+
+
+def feed_forward(core, groups, part, parts, mlp_low, final_low, w_up, w_down, down, grad, carried, tile=512):
+    count = mlp_low.shape[0]
+    width = w_up.shape[1] // parts
+    steps = width // tile
+    shift = part * steps
+    first = down is None
+    if first:
+        down = grad = jnp.zeros((8, 128), F32)
+    down_rows = D // (2 * groups)
+    up_rows = w_up.shape[1] // (2 * groups)
+    down_share = (groups // 4, 4, down_rows)
+    down_spec = pl.BlockSpec((*down_share, tile), lambda j, core: (0, 0, 0, j))
+    up_spec = pl.BlockSpec((tile // (2 * up_rows), up_rows, D), lambda j, core: (j, 0, 0))
+    whole = fixed_spec(count, D)
+    return run_kernel(
+        functools.partial(feed_forward_kernel, first=first),
+        (steps,),
+        [core],
+        [mlp_low, final_low, w_up, w_down, down, grad],
+        [
+            whole,
+            whole,
+            pl.BlockSpec((D, tile), lambda j, core: (0, shift + j)),
+            pl.BlockSpec((tile, D), lambda j, core: (shift + j, 0)),
+            fixed_spec(*down.shape),
+            fixed_spec(*down.shape),
+        ],
+        [down_spec, down_spec, up_spec, up_spec, whole, whole],
+        [shaped(BF16, *down_share, width)] * 2
+        + [shaped(BF16, groups // parts, up_rows, D)] * 2
+        + [shaped(F32, count, D)] * 2,
+        36,
+        "feed_forward",
+        scratch=[pltpu.VMEM((D, count), BF16), pltpu.VMEM((count, tile), BF16), pltpu.VMEM((count, tile), BF16)],
+        carried=carried,
+    )
+
+
+def middle_kernel(
+    length_ref, core_ref, down_ref, gmn_ref, res_ref, fin_ref, gain_ref, wo_ref, att_ref,
+    out_ref, low_ref, gatt_ref, gwo_keep_ref, gwo_away_ref, sums_ref, acc_ref
+):
+    step = pl.program_id(0)
+
+    @pl.when(step == 0)
+    def _():
+        sums_ref[...] = jnp.zeros_like(sums_ref)
+        acc_ref[...] = jnp.zeros_like(acc_ref)
+
+    residual = res_ref[...]
+    keep = valid_column(length_ref[0], residual.shape[0])
+    out_ref[...] = jnp.where(keep, residual + down_ref[...], 0.0).astype(BF16)
+    xhat, rstd = norm_rows(residual)
+    grad = gmn_ref[...]
+    add_column_sums(sums_ref, grad, xhat)
+    low = (fin_ref[...].astype(F32) + norm_rows_back(grad, xhat, rstd, gain_ref[...])).astype(BF16)
+    low_ref[...] = low
+    gatt_ref[...] = dot_nt(low, wo_ref[...]).astype(BF16)
+    acc_ref[...] += dot_tn(low, att_ref[...])
+
+    @pl.when(step == pl.num_programs(0) - 1)
+    def _():
+        share_out(core_ref[0], acc_ref[...], gwo_keep_ref, gwo_away_ref)
+
+
+def feed_forward_to_attention(
+    length, core, groups, down, grad_mlp_norm, residual, final_low, gain_row, w_out, attended, carried
+):
+    count = residual.shape[0]
+    row = row_spec(TOKEN_TILE, D)
+    share = (groups // 4, 4, D // (2 * groups), D)
+    return run_kernel(
+        middle_kernel,
+        (count // TOKEN_TILE,),
+        [length, core],
+        [down, grad_mlp_norm, residual, final_low, gain_row, w_out, attended],
+        [row, row, row, row, fixed_spec(1, D), fixed_spec(D, D), row],
+        [row, row, row, fixed_spec(*share), fixed_spec(*share), fixed_spec(8, D)],
+        [shaped(BF16, count, D)] * 3 + [shaped(BF16, *share)] * 2 + [shaped(F32, 8, D)],
+        15,
+        "feed_forward_to_attention",
+        scratch=[pltpu.VMEM((D, D), F32)],
+        carried=carried,
+    )
+
+
+def outer_kernel(core_ref, dq_ref, dk_ref, dv_ref, right_ref, keep_ref, away_ref, all_ref):
+    right = right_ref[...]
+    for group, ref in enumerate((dq_ref, dk_ref, dv_ref)):
+        for start in range(0, D, TOKEN_TILE):
+            rows = slice(group * D + start, group * D + start + TOKEN_TILE)
+            all_ref[rows, :] = dot_tn(ref[:, start : start + TOKEN_TILE], right).astype(BF16)
+    share_out(core_ref[0], all_ref[...], keep_ref, away_ref)
+
+
+def outer_qkv(core, groups, grads, right, half, carried):
+    count = right.shape[0]
+    columns = right.shape[1] // 2
+    share = (groups, 3 * D // (2 * groups), columns)
+    return run_kernel(
+        outer_kernel,
+        (1,),
+        [core],
+        [*grads, right],
+        [fixed_spec(count, D)] * 3 + [pl.BlockSpec((count, columns), lambda i, core: (0, half))],
+        [fixed_spec(*share)] * 2,
+        [shaped(BF16, *share)] * 2,
+        8,
+        "outer_qkv",
+        scratch=[pltpu.VMEM((3 * D, columns), BF16)],
+        carried=carried,
+    )
+
+
+def input_kernel(
+    core_ref, dq_ref, dk_ref, dv_ref, wqkv_ref, in_ref, low_ref, gain_ref, we_ref, emb_ref, nl_ref,
+    grad_ref, rows_ref, gwe_keep_ref, gwe_away_ref, sums_ref, acc_ref
+):
+    step = pl.program_id(0)
+
+    @pl.when(step == 0)
+    def _():
+        sums_ref[...] = jnp.zeros_like(sums_ref)
+        acc_ref[...] = jnp.zeros_like(acc_ref)
+
+    grad = (
+        dot_nt(dq_ref[...], wqkv_ref[:, :D])
+        + dot_nt(dk_ref[...], wqkv_ref[:, D : 2 * D])
+        + dot_nt(dv_ref[...], wqkv_ref[:, 2 * D :])
+    )
+    xhat, rstd = norm_rows(in_ref[...])
+    add_column_sums(sums_ref, grad, xhat)
+    low = (low_ref[...].astype(F32) + norm_rows_back(grad, xhat, rstd, gain_ref[...])).astype(BF16)
+    grad_ref[...] = low
+    acc_ref[...] += dot_tn(low, nl_ref[...])
+    back = dot_nt(low, we_ref[...])
+    emb = emb_ref[...].astype(F32)
+    emb_rstd = lax.rsqrt(jnp.mean(emb * emb, axis=-1, keepdims=True) + 1e-06)
+    normed = emb * emb_rstd
+    rows_ref[...] = (emb_rstd * (back - normed * jnp.mean(normed * back, axis=-1, keepdims=True))).astype(BF16)
+
+    @pl.when(step == pl.num_programs(0) - 1)
+    def _():
+        share_out(core_ref[0], acc_ref[...], gwe_keep_ref, gwe_away_ref)
+
+
+def input_gradient(core, groups, grads, w_qkv, inputs, residual_low, gain_row, w_embed, emb, normed_low, carried):
+    count = inputs.shape[0]
+    tile = TOKEN_TILE
+    share = (2 * groups, D // (4 * groups), EMB)
+    row, narrow = row_spec(tile, D), row_spec(tile, EMB)
+    return run_kernel(
+        input_kernel,
+        (count // tile,),
+        [core],
+        [*grads, w_qkv, inputs, residual_low, gain_row, w_embed, emb, normed_low],
+        [row, row, row, fixed_spec(D, 3 * D), row, row, fixed_spec(1, D), fixed_spec(EMB, D), narrow, narrow],
+        [row, narrow, fixed_spec(*share), fixed_spec(*share), fixed_spec(8, D)],
+        [shaped(BF16, count, D), shaped(BF16, count, EMB)] + [shaped(BF16, *share)] * 2 + [shaped(F32, 8, D)],
+        16,
+        "input_gradient",
+        scratch=[pltpu.VMEM((D, EMB), F32)],
+        carried=carried,
+    )
+
+
+def exchange(value, bit, dp_bits, pattern=1):
+    return lax.ppermute(value, "dp", [(i, i ^ (pattern << bit)) for i in range(1 << dp_bits)])
+
+
+class Halving:
+    def __init__(self, labels, dp_bits):
+        self.labels = list(labels)
+        self.dp_bits = dp_bits
+        self.keep = self.arrived = None
+
+    def over_cores(self, keep, away):
+        shape = (2,) * len(self.labels) + keep.shape[1:]
+        self.keep, self.arrived = keep.reshape(shape), swap_core(away).reshape(shape)
+
+    def total(self):
+        return self.arrived.astype(F32) + self.keep.astype(F32)
+
+    def halves(self, bit_label):
+        place = self.labels.index(bit_label)
+        bit = (lax.axis_index("dp") >> bit_label) & 1
+        self.labels.pop(place)
+
+        def half(which):
+            parts = (self.arrived, self.keep)
+            first, second = (lax.dynamic_index_in_dim(p, which, place, keepdims=False) for p in parts)
+            return (first.astype(F32) + second.astype(F32)).astype(BF16)
+
+        return half(bit), half(1 - bit)
+
+    def send(self, bit_label, keep, away):
+        self.keep, self.arrived = keep, exchange(away, bit_label, self.dp_bits)
+
+    def step(self, bit_label):
+        self.send(bit_label, *self.halves(bit_label))
+
+
+def whole_sequence_shards(
+    token_ids,
+    seq_lengths,
+    diffusion_time,
+    embed_table,
+    w_embed,
+    w_time,
+    gain_attn,
+    bias_attn,
+    gain_mlp,
+    bias_mlp,
+    w_qkv,
+    w_out,
+    w_up,
+    w_down,
+    cotangent,
+):
+    core = lax.axis_index("blk")
+    cores = core.reshape(1).astype(jnp.int32)
+    groups = lax.axis_size("dp")
+    devices = 2 * groups
+    dp_bits = groups.bit_length() - 1
+    everywhere = ("dp", "blk")
+    labels = list(reversed(range(dp_bits)))
+    planes = [[4 * high + low for low in range(4)] for high in range(groups // 4)]
+    lines = [[4 * high + low for high in range(groups // 4)] for low in range(4)]
+    ids = to_whole(core, token_ids)
+    cot = to_whole(core, cotangent)
+    positions = ids.shape[0]
+    length = lax.dynamic_index_in_dim(seq_lengths, core, 0, keepdims=True)
+    time = lax.dynamic_index_in_dim(diffusion_time, core, 0, keepdims=True)
+    emb = embed_table[ids]
+
+    valid = jnp.arange(positions, dtype=jnp.int32) < length[0]
+    row_count = VOCAB // devices
+    owner = jnp.where(valid, ids // row_count, -1)
+    offset = ids % row_count
+    slots = SLOT_ROWS - META_ROWS
+    member = owner[:, None] == jnp.arange(devices, dtype=jnp.int32)[None, :]
+    earlier = jnp.arange(positions)[:, None] > jnp.arange(positions)[None, :]
+    before = dot_nn(earlier.astype(BF16), member.astype(BF16))
+    rank = jnp.sum(jnp.where(member, before, 0.0), axis=1).astype(jnp.int32)
+    most = jnp.max(jnp.sum(member.astype(jnp.int32), axis=0))
+    offset_digits = jnp.stack(
+        [(offset // EXACT_BASE).astype(BF16), (offset % EXACT_BASE).astype(BF16), jnp.ones(positions, BF16)],
+        axis=1,
+    )
+
+    def dispatch(turn):
+        slot = rank - turn * slots
+        inside = (owner >= 0) & (slot >= 0) & (slot < slots)
+        target = jnp.where(inside, owner * SLOT_ROWS + META_ROWS + slot, -1)
+        place = jnp.arange(devices * SLOT_ROWS, dtype=jnp.int32)[:, None] == target[None, :]
+        digits = dot_nn(place.astype(BF16), offset_digits).reshape(devices, SLOT_ROWS, 3)
+        head = jnp.transpose(digits, (0, 2, 1)).reshape(devices, 1, 3 * SLOT_ROWS)
+        peak = jnp.stack([most // EXACT_BASE, most % EXACT_BASE]).astype(F32)
+        peak = jnp.broadcast_to(peak, (devices, 1, 2))
+        gap = jnp.zeros((devices, 1, EMB - 3 * SLOT_ROWS - 2), F32)
+        return target, jnp.concatenate([head, peak, gap], axis=2)
+
+    meta_target = jnp.arange(devices * META_ROWS, dtype=jnp.int32)
+    meta_target = meta_target // META_ROWS * SLOT_ROWS + meta_target % META_ROWS
+
+    def packed(target, meta, grads):
+        meta = meta.astype(BF16).reshape(devices * META_ROWS, EMB)
+        target = jnp.concatenate([target, meta_target])
+        place = jnp.arange(devices * SLOT_ROWS, dtype=jnp.int32)[:, None] == target[None, :]
+        rows = dot_nn(place.astype(BF16), jnp.concatenate([grads, meta]))
+        return rows.astype(BF16).reshape(devices, SLOT_ROWS, EMB)
+
+    def deliver(rows):
+        return lax.all_to_all(rows, everywhere, 0, 0, tiled=True)
+
+    def collect(rows):
+        head = rows[:, 0].astype(F32)
+        high, low, used = (head[:, i * SLOT_ROWS : (i + 1) * SLOT_ROWS] for i in range(3))
+        row = jnp.where(used > 0.5, high * EXACT_BASE + low, -1.0).astype(jnp.int32)
+        hit = jnp.arange(row_count, dtype=jnp.int32)[:, None] == row.reshape(1, -1)
+        return dot_nn(hit.astype(BF16), rows.reshape(-1, EMB))
+
+    first_target, first_head = dispatch(0)
+
+    def over_cores(keep, arrived):
+        return (keep.astype(F32) + arrived.astype(F32)).astype(BF16)
+
+    def scattered(value, index_groups):
+        return lax.psum_scatter(value, "dp", scatter_dimension=0, axis_index_groups=index_groups, tiled=True)[0]
+
+    time_low = time_features(time, TIME_WIDTH).astype(BF16)
+    modulation = dot_nn(time_low, w_time)
+    scale_attn, shift_attn, scale_mlp, shift_mlp = jnp.split(modulation, 4, axis=1)
+    gain_row_attn = gain_attn + scale_attn
+    gain_row_mlp = gain_mlp + scale_mlp
+    normed_low, inputs, attn_low, qkv = embed_and_project(
+        emb, w_embed, gain_row_attn, bias_attn + shift_attn, w_qkv
+    )
+    attended, lse = attend(length, qkv)
+    residual, mlp_low, final_low = attention_residual(
+        length, attended, inputs, w_out, gain_row_mlp, bias_mlp + shift_mlp, cot
+    )
+
+    top = dp_bits - 1
+    hidden_width = w_up.shape[1]
+    feed = functools.partial(feed_forward, cores, groups)
+    (keep_d, away_d, keep_u, away_u, down, grad), _ = feed(
+        0, 2, mlp_low, final_low, w_up, w_down, None, None, []
+    )
+    up_0, up_1 = Halving(labels[1:], dp_bits), Halving(labels[1:], dp_bits)
+    qkv_a, qkv_b = Halving(labels, dp_bits), Halving(labels, dp_bits)
+    up_0.over_cores(keep_u, away_u)
+    arrived_d = swap_core(away_d)
+    (next_keep, next_away, keep_u, away_u, down, grad), (up_0.keep, keep_d) = feed(
+        1, 2, mlp_low, final_low, w_up, w_down, down, grad, [up_0.keep, keep_d]
+    )
+    keep, away, down_0, next_keep, next_away, keep_u, away_u = behind(
+        *up_0.halves(0), over_cores(keep_d, arrived_d), next_keep, next_away, keep_u, away_u
+    )
+    up_0.send(0, keep, away)
+    up_1.over_cores(keep_u, away_u)
+    arrived_d = swap_core(next_away)
+    down_0 = scattered(down_0, lines)
+    (layer_out, residual_low, grad_att, keep_o, away_o, sums_mlp), kept = feed_forward_to_attention(
+        length, cores, groups, down, grad, residual, final_low, gain_row_mlp, w_out, attended,
+        [up_0.keep, up_1.keep, next_keep],
+    )
+    up_0.keep, up_1.keep, keep_d = kept
+    keep_0, away_0, keep_1, away_1, down_1, keep_o, away_o = behind(
+        *up_0.halves(1), *up_1.halves(0), over_cores(keep_d, arrived_d), keep_o, away_o
+    )
+    up_0.send(1, keep_0, away_0)
+    up_1.send(0, keep_1, away_1)
+    down_1 = scattered(down_1, lines)
+    arrived_o = swap_core(away_o)
+    back = functools.partial(attend_back, length, qkv, attended, grad_att, lse)
+    grads, (up_0.keep, up_1.keep, keep_o, down_0) = back(0, 2, [], [up_0.keep, up_1.keep, keep_o, down_0])
+    keep_0, away_0, keep_1, away_1, out_sum = behind(
+        *up_0.halves(2), *up_1.halves(1), over_cores(keep_o, arrived_o)
+    )
+    up_0.send(2, keep_0, away_0)
+    up_1.send(1, keep_1, away_1)
+    out_sum = scattered(out_sum, lines)
+    layer_out = to_split(core, layer_out)
+    grads, (up_0.keep, up_1.keep) = back(1, 2, grads, [up_0.keep, up_1.keep])
+    for bit in range(3, top):
+        up_0.step(bit)
+    keep_1, away_1 = behind(*up_1.halves(2))
+    up_1.send(2, keep_1, away_1)
+    for bit in range(3, top):
+        up_1.step(bit)
+    (keep_a, away_a), (up_0.keep, up_1.keep, down_1) = outer_qkv(
+        cores, groups, grads, attn_low, 0, [up_0.keep, up_1.keep, down_1]
+    )
+    zero_first, one_first = up_0.total().astype(BF16), up_1.total().astype(BF16)
+    top_bit = (lax.axis_index("dp") >> top) & 1
+    up_keep, up_away, keep_a, away_a = behind(
+        jnp.where(top_bit == 0, zero_first, one_first),
+        jnp.where(top_bit == 0, one_first, zero_first),
+        keep_a,
+        away_a,
+    )
+    up_away = exchange(up_away, top, dp_bits)
+    qkv_a.over_cores(keep_a, away_a)
+    orders = [list(range(dp_bits)), [1, 0] + list(range(2, dp_bits))]
+    (keep_b, away_b), (qkv_a.keep, up_keep) = outer_qkv(
+        cores, groups, grads, attn_low, 1, [qkv_a.keep, up_keep]
+    )
+    in_plane = jnp.concatenate([down_0, down_1, out_sum], axis=2)
+    keep_a, away_a, keep_b, away_b, in_plane = behind(*qkv_a.halves(orders[0][0]), keep_b, away_b, in_plane)
+    own_sum = scattered(in_plane, planes)
+    qkv_a.send(orders[0][0], keep_a, away_a)
+    qkv_b.over_cores(keep_b, away_b)
+    grad_w_up = (up_away.astype(F32) + up_keep.astype(F32)).T
+    qkv_b.send(orders[1][0], *behind(*qkv_b.halves(orders[1][0])))
+    (grad_input, grad_rows, keep_e, away_e, sums_attn), (qkv_a.keep, qkv_b.keep) = input_gradient(
+        cores, groups, grads, w_qkv, inputs, residual_low, gain_row_attn, w_embed, emb, normed_low,
+        [qkv_a.keep, qkv_b.keep],
+    )
+
+    grad_modulation = jnp.concatenate([sums_attn[0], sums_attn[1], sums_mlp[0], sums_mlp[1]])
+    gain_columns = jnp.transpose(grad_modulation.reshape(4, devices, -1), (1, 0, 2)).reshape(devices, -1)
+    mod_rows = jnp.concatenate([grad_modulation.reshape(devices, -1), gain_columns], axis=1)
+    mod_high = mod_rows.astype(BF16).astype(F32)
+    mod_low = mod_rows - mod_high
+    time_rows = jnp.broadcast_to(time_low.astype(F32), (devices, TIME_WIDTH))
+    first_meta = jnp.concatenate(
+        [first_head, jnp.stack([mod_high, mod_low, time_rows], axis=1)], axis=1
+    )
+    embed_rows = over_cores(keep_e, swap_core(away_e))
+    payload = jnp.concatenate([packed(first_target, first_meta, grad_rows), embed_rows], axis=1)
+    payload, keep_a, away_a, keep_b, away_b = behind(
+        payload, *qkv_a.halves(orders[0][1]), *qkv_b.halves(orders[1][1])
+    )
+    arrived = deliver(payload)
+    qkv_a.send(orders[0][1], keep_a, away_a)
+    qkv_b.send(orders[1][1], keep_b, away_b)
+    grad_w_qkv = jnp.concatenate([qkv_a.total(), qkv_b.total()], axis=-1).astype(BF16)
+    grad_w_qkv = grad_w_qkv.reshape(groups // 4, -1, D)
+    plane = lax.axis_index("dp") >> 2
+    parts = [lax.dynamic_index_in_dim(grad_w_qkv, plane, 0, keepdims=False)]
+    for step in range(1, groups // 4):
+        away = lax.dynamic_index_in_dim(grad_w_qkv, plane ^ step, 0, keepdims=False)
+        parts.append(exchange(away, 2, dp_bits, step))
+    grad_w_qkv = sum(part.astype(F32) for part in parts)
+    embed_sum = arrived[:, SLOT_ROWS:].astype(F32).reshape(groups, -1, EMB)
+    embed_sum = jnp.sum(embed_sum, axis=0)
+    arrived = arrived[:, :SLOT_ROWS]
+    grad_input = to_split(core, grad_input)
+    grad_table = collect(arrived)
+    sums = arrived[:, 1].astype(F32) + arrived[:, 2].astype(F32)
+    time_width = sums.shape[1] // 2
+    grad_w_time = lax.dot_general(
+        arrived[:, 3].astype(F32),
+        sums[:, :time_width],
+        (((0,), (0,)), ((), ())),
+        precision=lax.Precision.HIGHEST,
+    )
+    gain_sums = jnp.sum(sums[:, time_width:], axis=0).reshape(4, -1)
+    peaks = arrived[:, 0, 3 * SLOT_ROWS : 3 * SLOT_ROWS + 2].astype(F32)
+    peak = jnp.max(peaks[:, 0] * EXACT_BASE + peaks[:, 1]).astype(jnp.int32)
+    turns = (peak + slots - 1) // slots
+
+    def more_turns(state):
+        return state[0] < turns
+
+    def next_turn(state):
+        turn, table = state
+        target, head = dispatch(turn)
+        meta = jnp.pad(head, ((0, 0), (0, META_ROWS - 1), (0, 0)))
+        return turn + 1, table + collect(deliver(packed(target, meta, grad_rows)))
+
+    _, grad_table = lax.while_loop(more_turns, next_turn, (jnp.int32(1), grad_table))
+    return (
+        layer_out,
+        grad_input,
+        grad_table,
+        embed_sum.T,
+        grad_w_time,
+        gain_sums[0],
+        gain_sums[1],
+        gain_sums[2],
+        gain_sums[3],
+        grad_w_qkv.T,
+        own_sum[:, hidden_width:].astype(F32).T,
+        grad_w_up,
+        own_sum[:, :hidden_width].astype(F32).T,
+    )
+
+
+def shards(*arguments):
+    seq_count, pos_count = arguments[0].shape
+    groups = lax.axis_size("dp")
+    whole = seq_count == 2 and lax.axis_size("blk") == 2
+    whole = whole and groups >= 4 and groups & (groups - 1) == 0 and pos_count % 256 == 0
+    return whole_sequence_shards(*arguments) if whole else split_position_shards(*arguments)
 
 
 def solution(mesh):

time: 1480 us -> 435 us (0.29)
  waiting for transfers between devices: 571 us -> 47.3 us
  matrix products: 369 us -> 9.09 us
  Pallas kernels: 0 us -> 230 us
  other arithmetic: 223 us -> 61 us
  local copies, waits for them, and re-layouts: 187 us -> 34.5 us
  blocking collectives: 106 us -> 0 us
  starting transfers between devices: 2.44 us -> 26.3 us
    reduce_scatter x10 -> x3, waiting for transfers between devices: 431 us -> 0.02 us  [scattered(): lax.psum_scatter(value, 'dp', scatter_dimension=0, axis_index_groups=inde...]
    dot_general x29 -> x6, matrix products: 369 us -> 9.09 us  [the longest x5 8.17 us: dot_nn(): lax.dot_general(left, right, (((1,), (0,)), ((), ())), preferred_element_...]
    pallas_call x0 -> x19, Pallas kernels: none -> 230 us  [the longest x9 182 us: run_kernel(): pl.pallas_call(kernel, grid_spec=pltpu.PrefetchScalarGridSpec(num_scalar_...]
    scatter-add x1 -> x0, other arithmetic: 161 us -> none  [scatter_rows(): running_total.at[jnp.where(inside, offsets, row_span)]]
    all_gather x2 -> x0, waiting for transfers between devices: 115 us -> none  [the longest x1 115 us: shards(): lax.all_gather(flat_grads.astype(jnp.bfloat16), ('dp', 'blk'), axis=0, ti...]
    unnamed x173 -> x71, local copies, waits for them, and re-layouts: 86.1 us -> 6.1 us
    unnamed x1 -> x0, blocking collectives: 71 us -> none
    slice x11 -> x5, local copies, waits for them, and re-layouts: 51.7 us -> 2.41 us  [the longest x1 0.86 us: whole_sequence_shards(): sums_attn[0]]
  transfers between devices with their start and end apart: 21 -> 31, of which waited for: 8 -> 7; matrix products, arithmetic and copies ran while one was open for 23% -> 21% of each run, Pallas kernels for 0% -> 43%
where the time goes in v1:
time: 435 us; the launch traced here: 427 us
  Pallas kernels  230 us (53%)
  other arithmetic  61 us (14%)
  waiting for transfers between devices  47.3 us (11%)
  local copies, waits for them, and re-layouts  34.5 us (8%)
  starting transfers between devices  26.3 us (6%)
  between operations  18.5 us (4%)
  matrix products  9.09 us (2%)
    pallas_call x9, Pallas kernels, run_kernel(): pl.pallas_call(kernel, grid_spec=pltpu.PrefetchScalarGridSpec(num_scalar_...  182 us
    pallas_call x2, Pallas kernels, attend_back(): pl.pallas_call(kernel, grid_spec=pltpu.PrefetchScalarGridSpec(num_scalar_...  48.7 us
    ppermute x14, waiting for transfers between devices, exchange(): lax.ppermute(value, 'dp', [(i, i ^ pattern << bit) for i in range(1 << dp...  47.2 us
    convert_element_type x10, other arithmetic, half(): return (first.astype(F32) + second.astype(F32)).astype(BF16)  29.4 us
    ppermute x14, starting transfers between devices, exchange(): lax.ppermute(value, 'dp', [(i, i ^ pattern << bit) for i in range(1 << dp...  19.8 us
    gather x1, local copies, waits for them, and re-layouts, whole_sequence_shards(): emb = embed_table[ids]  12.4 us
  transfers between devices with their start and end apart: 31, of which 7 were waited for; matrix products, arithmetic and copies ran while one was open for 21% of the time, Pallas kernels for 43%

profile of v1, /device:TPU:8, one launch (start us, length us, event | category | flops | bytes accessed | tf_op | source)
XLA Modules:
  0.0 427.1 jit_solution(4505881762226768489)
XLA Ops:
  14.0 12.4 %gather_fusion = bf16[1024,256]{1,0:T(8,128)(2,1)} fusion(bf16[32000,256]{1,0:T(8,128)(2,1)} %param.20, s32[1024]{0:T(1024)S(1)} %broadcast_clamp_fusion), kind=kCustom, calls=%fused_computation | custom fusion | bytes 1052672 | tf_op jit(solution)/shard_map/gather | solution.py:970
  26.4 13.7 %embed_and_project.1 = (bf16[1024,256]{1,0:T(8,128)(2,1)}, f32[1024,1024]{1,0:T(8,128)}, bf16[1024,1024]{1,0:T(8,128)(2,1)}, bf16[1024,3072]{1,0:T(8,128)(2,1)}) custom-call(bf16[1024,256]{1,0:T(8,128)(2,1)} %gather_fusion, bf16[256,1024]{1,0:T(8,128)(2,1)} %refs_8_.1, f32[1,1024]{1,0:T(1,128)} %get-tuple-element.696.refs_2_.refs_7_, ...), custom_call_target="tpu_custom_call" | custom-call | flops 3600000000 | bytes 1024 | tf_op jit(solution)/shard_map/embed_and_project/pallas_call | solution.py:506
  40.1 30.5 %attend.1 = (bf16[1024,1024]{1,0:T(8,128)(2,1)}, f32[8,2,1024]{2,1,0:T(2,128)}) custom-call(s32[1]{0:T(128)} %dynamic_slice.172.refs_0_, bf16[1024,3072]{1,0:T(8,128)(2,1)} %get-tuple-element.415.refs_1_.refs_2_.refs_3_, bf16[1024,3072]{1,0:T(8,128)(2,1)} %get-tuple-element.415.refs_1_.refs_2_.refs_3_, ...), custom_call_target="tpu_custom_call" | custom-call | flops 8999999488 | bytes 1024 | tf_op jit(solution)/shard_map/attend/pallas_call | solution.py:506
  72.2 10.1 %attention_residual.1 = (f32[1024,1024]{1,0:T(8,128)}, bf16[1024,1024]{1,0:T(8,128)(2,1)}, bf16[1024,1024]{1,0:T(8,128)(2,1)}) custom-call(s32[1]{0:T(128)} %dynamic_slice.172.refs_0_, bf16[1024,1024]{1,0:T(8,128)(2,1)} %get-tuple-element.416.refs_1_.refs_8_.refs_4_, f32[1024,1024]{1,0:T(8,128)} %get-tuple-element.417.refs_2_.refs_5_, ...), custom_call_target="tpu_custom_call" | custom-call | flops 2400000000 | bytes 1024 | tf_op jit(solution)/shard_map/attention_residual/pallas_call | solution.py:506
  82.9 38.0 %feed_forward.2 = (bf16[4,4,32,2048]{3,2,1,0:T(8,128)(2,1)}, bf16[4,4,32,2048]{3,2,1,0:T(8,128)(2,1)}, bf16[8,128,1024]{2,1,0:T(8,128)(2,1)}, bf16[8,128,1024]{2...) custom-call(s32[1]{0:T(128)} %bitcast.refs_0_.refs_1_, bf16[1024,1024]{1,0:T(8,128)(2,1)} %get-tuple-element.418.refs_1_, ...), custom_call_target="tpu_custom_call" | custom-call | flops 10800000000 | bytes 1024 | tf_op jit(solution)/shard_map/feed_forward/pallas_call | solution.py:506
  121.5 39.7 %feed_forward.3 = (bf16[4,4,32,2048]{3,2,1,0:T(8,128)(2,1)}, bf16[4,4,32,2048]{3,2,1,0:T(8,128)(2,1)}, bf16[8,128,1024]{2,1,0:T(8,128)(2,1)}, bf16[8,128,1024]{2...) custom-call(s32[1]{0:T(128)} %bitcast.refs_0_.refs_1_, ...), custom_call_target="tpu_custom_call", output_to_operand_aliasing={{6}: (7, {}), {7}: (8, {})} | custom-call | flops 10800000000 | bytes 1024 | tf_op jit(solution)/shard_map/feed_forward/pallas_call | solution.py:506
  161.2 4.8 %fusion.31 = (bf16[2,2,128,1024]{3,2,1,0:T(8,128)(2,1)}, bf16[2,2,128,1024]{3,2,1,0:T(8,128)(2,1)}) fusion(s32[]{:T(128)S(6)} %select_n.305, bf16[2,2,2,128,1024]{4,3,2,1,0:T(8,128)(2,1)} %bitcast.15, s32[]{:T(128)S(6)} %select_n.304, bf16[2,2,2,128,1024]{4,3,2,1,0:T(8,128)(2,1)} %get-tuple-element.428), kind=kLoop, calls=%fused_computation.76 | loop fusion | flops 4194304 | bytes 6291464 | tf_op jit(solution)/shard_map/convert_element_type | solution.py:928
  171.9 16.0 %feed_forward_to_attention.1 = (bf16[1024,1024]{1,0:T(8,128)(2,1)}, bf16[1024,1024]{1,0:T(8,128)(2,1)}, bf16[1024,1024]{1,0:T(8,128)(2,1)}, bf16[4,4,32,1024]{3,...) custom-call(s32[1]{0:T(128)} %dynamic_slice.172.refs_0_, ...), custom_call_target="tpu_custom_call", output_to_operand_aliasing={{6}: (9, {}), {7}: (10, {}), {8}: (11, {})} | custom-call | flops 4499999744 | bytes 1024 | tf_op jit(solution)/shard_map/feed_forward_to_attention/pallas_call | solution.py:506
  187.9 7.8 %collective-permute-done.5 = bf16[2,2,128,1024]{3,2,0,1:T(8,128)(2,1)S(1)} collective-permute-done((bf16[2,2,128,1024]{3,2,0,1:T(8,128)(2,1)}, bf16[2,2,128,1024]{3,2,0,1:T(8,128)(2,1)S(1)}, u32[]{:S(2)}, u32[]{:S(2)}) %collective-permute-start.5) | collective-permute-done | bytes 1048608 | tf_op jit(solution)/shard_map/ppermute | solution.py:904
  198.3 4.1 fusion.33
  202.4 3.7 add_convert_fusion.refs_4_
  212.4 24.1 %attend_back.2 = (bf16[1024,1024]{1,0:T(8,128)(2,1)}, bf16[1024,1024]{1,0:T(8,128)(2,1)}, bf16[1024,1024]{1,0:T(8,128)(2,1)}, bf16[2,128,1024]{2,1,0:T(8,128)(2,...) custom-call(s32[1]{0:T(128)} %dynamic_slice.172.refs_0_, ...), custom_call_target="tpu_custom_call", output_to_operand_aliasing={{3}: (7, {}), {4}: (8, {}), {5}: (9, {}), {6}: (10, {})} | custom-call | flops 6899999744 | bytes 1024 | tf_op jit(solution)/shard_map/attend_back/pallas_call | solution.py:594
  247.9 24.6 %attend_back.3 = (bf16[1024,1024]{1,0:T(8,128)(2,1)}, bf16[1024,1024]{1,0:T(8,128)(2,1)}, bf16[1024,1024]{1,0:T(8,128)(2,1)}, bf16[128,1024]{1,0:T(8,128)(2,1)}, bf16[2,128,1024]{2,1,0:T(8,128)(2,1)}) custom-call(s32[1]{0:T(128)} %dynamic_slice.172.refs_0_, ...), custom_call_target="tpu_custom_call", output_to_operand_aliasing={{0}: (7, {}), {1}: (8, {}), {2}: (9, {}), {3}: (10, {}), {4... | custom-call | flops 6899999744 | bytes 1024 | tf_op jit(solution)/shard_map/attend_back/pallas_call | solution.py:594
  278.0 8.3 %outer_qkv.2 = (bf16[16,96,512]{2,1,0:T(8,128)(2,1)}, bf16[16,96,512]{2,1,0:T(8,128)(2,1)}, bf16[128,1024]{1,0:T(8,128)(2,1)}, bf16[128,1024]{1,0:T(8,128)(2,1)}, bf16[4,32,2048]{2,1,0:T(8,128)(2,1)}) custom-call(s32[1]{0:T(128)} %bitcast.refs_0_.refs_1_, ...), custom_call_target="tpu_custom_call", output_to_operand_aliasing={{2}: (5, {}), {3}: (6, {}), {4}: (7, {})} | custom-call | flops 2400000000 | bytes 1024 | tf_op jit(solution)/shard_map/outer_qkv/pallas_call | solution.py:506
  286.3 5.0 %collective-permute-done.13 = bf16[128,1024]{1,0:T(8,128)(2,1)S(1)} collective-permute-done((bf16[128,1024]{1,0:T(8,128)(2,1)}, bf16[128,1024]{1,0:T(8,128)(2,1)S(1)}, u32[]{:S(2)}, u32[]{:S(2)}) %collective-permute-start.13) | collective-permute-done | bytes 262176 | tf_op jit(solution)/shard_map/ppermute | solution.py:904
  296.0 8.3 %outer_qkv.3 = (bf16[16,96,512]{2,1,0:T(8,128)(2,1)}, bf16[16,96,512]{2,1,0:T(8,128)(2,1)}, bf16[2,2,2,2,96,512]{5,4,3,2,1,0:T(8,128)(2,1)}, bf16[128,1024]{1,0:T(8,128)(2,1)}) custom-call(s32[1]{0:T(128)} %bitcast.refs_0_.refs_1_, bf16[1024,1024]{1,0:T(8,128)(2,1)} %get-tuple-element.464.refs_1_, ...), custom_call_target="tpu_custom_call", output_to_operand_aliasing={{2}: (5, {}), {3}: (6, {})} | custom-call | flops 2400000000 | bytes 1024 | tf_op jit(solution)/shard_map/outer_qkv/pallas_call | solution.py:506
  316.3 4.4 %collective-permute-start.25 = (bf16[128,1024]{1,0:T(8,128)(2,1)S(1)}, bf16[128,1024]{1,0:T(8,128)(2,1)}, u32[]{:S(2)}, u32[]{:S(2)}) collective-permute-start(bf16[128,1024]{1,0:T(8,128)(2,1)S(1)} %copy-done.23), channel_id=1, source_target_pairs={{0,16},{2,18},{4,20},{6,22},{8,24},{10,26},{12,28},{14,30},{16,0},... | collective-permute-start | bytes 786440 | tf_op jit(solution)/shard_map/ppermute | solution.py:904
  321.8 3.5 fusion.41
  327.8 17.0 %input_gradient.1 = (bf16[1024,1024]{1,0:T(8,128)(2,1)}, bf16[1024,256]{1,0:T(8,128)(2,1)}, bf16[32,16,256]{2,1,0:T(8,128)(2,1)}, bf16[32,16,256]{2,1,0:T(8,128)...) custom-call(s32[1]{0:T(128)} %bitcast.refs_0_.refs_1_, ...), custom_call_target="tpu_custom_call", output_to_operand_aliasing={{5}: (11, {}), {6}: (12, {})} | custom-call | flops 4800000000 | bytes 1024 | tf_op jit(solution)/shard_map/input_gradient/pallas_call | solution.py:506
  346.2 3.1 fusion.26
  356.8 3.8 all-to-all-start.1
  371.7 13.5 %collective-permute-done.21 = bf16[2,2,96,512]{3,2,1,0:T(8,128)(2,1)S(1)} collective-permute-done((bf16[2,2,96,512]{3,2,1,0:T(8,128)(2,1)S(1)}, bf16[2,2,96,512]{3,2,1,0:T(8,128)(2,1)S(1)}, u32[]{:S(2)}, u32[]{:S(2)}) %collective-permute-start.21) | collective-permute-done | bytes 393248 | tf_op jit(solution)/shard_map/ppermute | solution.py:904
  393.8 11.3 %collective-permute-done.23 = bf16[96,1024]{1,0:T(8,128)(2,1)S(1)} collective-permute-done((bf16[96,1024]{1,0:T(8,128)(2,1)S(1)}, bf16[96,1024]{1,0:T(8,128)(2,1)S(1)}, u32[]{:S(2)}, u32[]{:S(2)}) %collective-permute-start.23) | collective-permute-done | bytes 196640 | tf_op jit(solution)/shard_map/ppermute | solution.py:904
  405.1 6.3 %collective-permute-done.24 = bf16[96,1024]{1,0:T(8,128)(2,1)S(1)} collective-permute-done((bf16[96,1024]{1,0:T(8,128)(2,1)S(1)}, bf16[96,1024]{1,0:T(8,128)(2,1)S(1)}, u32[]{:S(2)}, u32[]{:S(2)}) %collective-permute-start.24) | collective-permute-done | bytes 196640 | tf_op jit(solution)/shard_map/ppermute | solution.py:904
  (234 shorter events, 94.6 us)
Async XLA Ops:
  7.2 205.2 %reduce-scatter.7.cloned.1.call-start = ((), (), s32[]{:S(2)}) async-start(), calls=%async_computation.6 | async-start | bytes 2621440 | tf_op jit(solution)/shard_map/reduce_scatter | solution.py:1025
  10.5 60.1 %collective-permute-start.1 = (bf16[512,1024]{1,0:T(8,128)(2,1)}, bf16[512,1024]{1,0:T(8,128)(2,1)S(1)}, u32[]{:S(2)}, u32[]{:S(2)}) collective-permute-start(bf16[512,1024]{1,0:T(8,128)(2,1)} %dynamic-slice_bitcast_fusion.2), channel_id=1, source_target_pairs={{0,1},{1,0},{2,3},{3,2},{4,5},{5,4},{6,7},{7,6},{8,9},{9,8},{10,11... | collective-permute-start | bytes 3145736 | tf_op jit(solution)/shard_map/ppermute | solution.py:464
  120.9 40.3 %collective-permute-start.2 = (bf16[8,128,1024]{2,1,0:T(8,128)(2,1)}, bf16[8,128,1024]{2,1,0:T(8,128)(2,1)}, u32[]{:S(2)}, u32[]{:S(2)}) collective-permute-start(bf16[8,128,1024]{2,1,0:T(8,128)(2,1)} %get-tuple-element.427), channel_id=1, source_target_pairs={{0,1},{1,0},{2,3},{3,2},{4,5},{5,4},{6,7},{7,6},{8,9},{9,8},{10,11... | collective-permute-start | bytes 6291464 | tf_op jit(solution)/shard_map/ppermute | solution.py:464
  121.0 45.0 %collective-permute-start.3 = (bf16[4,4,32,2048]{3,2,1,0:T(8,128)(2,1)}, bf16[4,4,32,2048]{3,2,1,0:T(8,128)(2,1)S(1)}, u32[]{:S(2)}, u32[]{:S(2)}) collective-permute-start(bf16[4,4,32,2048]{3,2,1,0:T(8,128)(2,1)} %get-tuple-element.430), channel_id=1, source_target_pairs={{0,1},{1,0},{2,3},{3,2},{4,5},{5,4},{6,7},{7,6},{8,9},{9,8},{10,11... | collective-permute-start | bytes 6291464 | tf_op jit(solution)/shard_map/ppermute | solution.py:464
  168.2 109.8 %reduce-scatter.9.cloned.1.call-start = ((), (), s32[]{:S(2)}) async-start(), calls=%async_computation.7 | async-start | bytes 2621440 | tf_op jit(solution)/shard_map/reduce_scatter | solution.py:1025
  168.2 30.1 %collective-permute-start.6 = (bf16[8,128,1024]{2,1,0:T(8,128)(2,1)}, bf16[8,128,1024]{2,1,0:T(8,128)(2,1)}, u32[]{:S(2)}, u32[]{:S(2)}) collective-permute-start(bf16[8,128,1024]{2,1,0:T(8,128)(2,1)} %get-tuple-element.443), channel_id=1, source_target_pairs={{0,1},{1,0},{2,3},{3,2},{4,5},{5,4},{6,7},{7,6},{8,9},{9,8},{10,11... | collective-permute-start | bytes 6291464 | tf_op jit(solution)/shard_map/ppermute | solution.py:464
  168.3 34.1 %collective-permute-start.7 = (bf16[4,4,32,2048]{3,2,1,0:T(8,128)(2,1)}, bf16[4,4,32,2048]{3,2,1,0:T(8,128)(2,1)}, u32[]{:S(2)}, u32[]{:S(2)}) collective-permute-start(bf16[4,4,32,2048]{3,2,1,0:T(8,128)(2,1)} %get-tuple-element.446), channel_id=1, source_target_pairs={{0,1},{1,0},{2,3},{3,2},{4,5},{5,4},{6,7},{7,6},{8,9},{9,8},{10,11... | collective-permute-start | bytes 6291464 | tf_op jit(solution)/shard_map/ppermute | solution.py:464
  170.4 25.4 %collective-permute-start.5 = (bf16[2,2,128,1024]{3,2,0,1:T(8,128)(2,1)}, bf16[2,2,128,1024]{3,2,0,1:T(8,128)(2,1)S(1)}, u32[]{:S(2)}, u32[]{:S(2)}) collective-permute-start(bf16[2,2,128,1024]{3,2,0,1:T(8,128)(2,1)} %copy.227), channel_id=1, source_target_pairs={{0,2},{2,0},{4,6},{6,4},{8,10},{10,8},{12,14},{14,12},{16,18},{18,... | collective-permute-start | bytes 3145736 | tf_op jit(solution)/shard_map/ppermute | solution.py:904
  206.1 98.1 %reduce-scatter.11.cloned.1.call-start = ((), (), s32[]{:S(2)}) async-start(), calls=%async_computation.8 | async-start | bytes 1310720 | tf_op jit(solution)/shard_map/reduce_scatter | solution.py:1025
  208.4 31.2 %collective-permute-start.9 = (bf16[2,2,128,1024]{3,2,0,1:T(8,128)(2,1)}, bf16[2,2,128,1024]{3,2,0,1:T(8,128)(2,1)}, u32[]{:S(2)}, u32[]{:S(2)}) collective-permute-start(bf16[2,2,128,1024]{3,2,0,1:T(8,128)(2,1)} %copy.234), channel_id=1, source_target_pairs={{0,2},{2,0},{4,6},{6,4},{8,10},{10,8},{12,14},{14,12},{16,18},{18,... | collective-permute-start | bytes 3145736 | tf_op jit(solution)/shard_map/ppermute | solution.py:904
  210.7 31.5 %collective-permute-start.10 = (bf16[4,4,32,1024]{3,2,1,0:T(8,128)(2,1)S(1)}, bf16[4,4,32,1024]{3,2,1,0:T(8,128)(2,1)}, u32[]{:S(2)}, u32[]{:S(2)}) collective-permute-start(bf16[4,4,32,1024]{3,2,1,0:T(8,128)(2,1)S(1)} %copy-done.24), channel_id=1, source_target_pairs={{0,1},{1,0},{2,3},{3,2},{4,5},{5,4},{6,7},{7,6},{8,9},{9,8},{10,11... | collective-permute-start | bytes 3145736 | tf_op jit(solution)/shard_map/ppermute | solution.py:464
  210.8 25.7 %collective-permute-start.8 = (bf16[2,128,1024]{2,1,0:T(8,128)(2,1)S(1)}, bf16[2,128,1024]{2,1,0:T(8,128)(2,1)S(1)}, u32[]{:S(2)}, u32[]{:S(2)}) collective-permute-start(bf16[2,128,1024]{2,1,0:T(8,128)(2,1)S(1)} %copy-done.15), channel_id=1, source_target_pairs={{0,4},{2,6},{4,0},{6,2},{8,12},{10,14},{12,8},{14,10},{16,20},{18,... | collective-permute-start | bytes 1572872 | tf_op jit(solution)/shard_map/ppermute | solution.py:904
  244.9 27.6 %collective-permute-start.12 = (bf16[2,128,1024]{2,1,0:T(8,128)(2,1)}, bf16[2,128,1024]{2,1,0:T(8,128)(2,1)S(1)}, u32[]{:S(2)}, u32[]{:S(2)}) collective-permute-start(bf16[2,128,1024]{2,1,0:T(8,128)(2,1)} %get-tuple-element.472), channel_id=1, source_target_pairs={{0,4},{2,6},{4,0},{6,2},{8,12},{10,14},{12,8},{14,10},{16,20},{18,... | collective-permute-start | bytes 1572872 | tf_op jit(solution)/shard_map/ppermute | solution.py:904
  245.4 40.9 %collective-permute-start.11 = (bf16[128,1024]{1,0:T(8,128)(2,1)}, bf16[128,1024]{1,0:T(8,128)(2,1)S(1)}, u32[]{:S(2)}, u32[]{:S(2)}) collective-permute-start(bf16[128,1024]{1,0:T(8,128)(2,1)} %get-tuple-element.469), channel_id=1, source_target_pairs={{0,8},{2,10},{4,12},{6,14},{8,0},{10,2},{12,4},{14,6},{16,24},{18,... | collective-permute-start | bytes 786440 | tf_op jit(solution)/shard_map/ppermute | solution.py:904
  247.9 120.3 %reduce-scatter.13.cloned.1.call-start = ((), (), s32[]{:S(2)}) async-start(), calls=%async_computation.9 | async-start | bytes 1638400
  296.0 17.1 %collective-permute-start.4 = (bf16[512,1024]{1,0:T(8,128)(2,1)}, bf16[512,1024]{1,0:T(8,128)(2,1)}, u32[]{:S(2)}, u32[]{:S(2)}) collective-permute-start(bf16[512,1024]{1,0:T(8,128)(2,1)} %dynamic-slice_bitcast_fusion.1), channel_id=1, source_target_pairs={{0,1},{1,0},{2,3},{3,2},{4,5},{5,4},{6,7},{7,6},{8,9},{9,8},{10,11... | collective-permute-start | bytes 3145736 | tf_op jit(solution)/shard_map/ppermute | solution.py:464
  316.3 46.8 %collective-permute-start.25 = (bf16[128,1024]{1,0:T(8,128)(2,1)S(1)}, bf16[128,1024]{1,0:T(8,128)(2,1)}, u32[]{:S(2)}, u32[]{:S(2)}) collective-permute-start(bf16[128,1024]{1,0:T(8,128)(2,1)S(1)} %copy-done.23), channel_id=1, source_target_pairs={{0,16},{2,18},{4,20},{6,22},{8,24},{10,26},{12,28},{14,30},{16,0},... | collective-permute-start | bytes 786440 | tf_op jit(solution)/shard_map/ppermute | solution.py:904
  320.8 28.5 %collective-permute-start.18 = (bf16[2,2,2,96,512]{4,3,1,0,2:T(8,128)(2,1)S(1)}, bf16[2,2,2,96,512]{4,3,1,0,2:T(8,128)(2,1)}, u32[]{:S(2)}, u32[]{:S(2)}) collective-permute-start(bf16[2,2,2,96,512]{4,3,1,0,2:T(8,128)(2,1)S(1)} %copy.251), channel_id=1, source_target_pairs={{0,2},{2,0},{4,6},{6,4},{8,10},{10,8},{12,14},{14,12},{16,18},{18,... | collective-permute-start | bytes 2359304 | tf_op jit(solution)/shard_map/ppermute | solution.py:904
  327.4 27.2 %collective-permute-start.19 = (bf16[2,2,2,96,512]{4,3,1,0,2:T(8,128)(2,1)}, bf16[2,2,2,96,512]{4,3,1,0,2:T(8,128)(2,1)}, u32[]{:S(2)}, u32[]{:S(2)}) collective-permute-start(bf16[2,2,2,96,512]{4,3,1,0,2:T(8,128)(2,1)} %copy.254), channel_id=1, source_target_pairs={{0,4},{2,6},{4,0},{6,2},{8,12},{10,14},{12,8},{14,10},{16,20},{18,... | collective-permute-start | bytes 2359304 | tf_op jit(solution)/shard_map/ppermute | solution.py:904
  356.8 55.4 %all-to-all-start.1 = ((bf16[32,88,256]{2,1,0:T(8,128)(2,1)}), bf16[32,88,256]{2,1,0:T(8,128)(2,1)S(1)}, u32[]{:S(2)}, u32[]{:S(2)}) async-start(bf16[32,88,256]{2,1,0:T(8,128)(2,1)} %get-tuple-element.504), calls=%async_computation.4 | async-start | bytes 2883584 | tf_op jit(solution)/shard_map/all_to_all | solution.py:1010
  365.2 20.0 %collective-permute-start.21 = (bf16[2,2,96,512]{3,2,1,0:T(8,128)(2,1)S(1)}, bf16[2,2,96,512]{3,2,1,0:T(8,128)(2,1)S(1)}, u32[]{:S(2)}, u32[]{:S(2)}) collective-permute-start(bf16[2,2,96,512]{3,2,1,0:T(8,128)(2,1)S(1)} %copy-done.22), channel_id=1, source_target_pairs={{0,2},{2,0},{4,6},{6,4},{8,10},{10,8},{12,14},{14,12},{16,18},{18,... | collective-permute-start | bytes 1179656 | tf_op jit(solution)/shard_map/ppermute | solution.py:904
  366.6 18.6 %collective-permute-start.20 = (bf16[2,2,96,512]{3,2,1,0:T(8,128)(2,1)S(1)}, bf16[2,2,96,512]{3,2,1,0:T(8,128)(2,1)S(1)}, u32[]{:S(2)}, u32[]{:S(2)}) collective-permute-start(bf16[2,2,96,512]{3,2,1,0:T(8,128)(2,1)S(1)} %copy-done.21), channel_id=1, source_target_pairs={{0,4},{2,6},{4,0},{6,2},{8,12},{10,14},{12,8},{14,10},{16,20},{18,... | collective-permute-start | bytes 1179656 | tf_op jit(solution)/shard_map/ppermute | solution.py:904
  386.3 18.7 %collective-permute-start.23 = (bf16[96,1024]{1,0:T(8,128)(2,1)S(1)}, bf16[96,1024]{1,0:T(8,128)(2,1)S(1)}, u32[]{:S(2)}, u32[]{:S(2)}) collective-permute-start(bf16[96,1024]{1,0:T(8,128)(2,1)S(1)} %get-tuple-element.687), channel_id=1, source_target_pairs={{0,16},{2,18},{4,20},{6,22},{8,24},{10,26},{12,28},{14,30},{16,0},... | collective-permute-start | bytes 589832 | tf_op jit(solution)/shard_map/ppermute | solution.py:904
  388.6 22.8 %collective-permute-start.24 = (bf16[96,1024]{1,0:T(8,128)(2,1)S(1)}, bf16[96,1024]{1,0:T(8,128)(2,1)S(1)}, u32[]{:S(2)}, u32[]{:S(2)}) collective-permute-start(bf16[96,1024]{1,0:T(8,128)(2,1)S(1)} %get-tuple-element.688), channel_id=1, source_target_pairs={{0,24},{2,26},{4,28},{6,30},{8,16},{10,18},{12,20},{14,22},{16,8},... | collective-permute-start | bytes 589832 | tf_op jit(solution)/shard_map/ppermute | solution.py:904
  (41 other events, 259.7 us)
Sparse Core Ops, SparseCore 0:
  168.3 42.8 reduce-scatter.6
  213.5 47.6 reduce-scatter.8
  263.5 32.6 reduce-scatter.10
  321.9 35.3 reduce-scatter.12
